TPU v7x, 32 devices: a whole 2x2x4 slice. The times are simulated.
32 devices in a mesh: fsdp: 16 (over z, y, core), tp: 2 (over x).
Axes of the slice: x: 2, y: 2, z: 4, core: 2. Of those that a mesh axis runs over, the one named last changes fastest.
Arguments:
- tokens: bfloat16 [16384, 1024], P(('fsdp', 'tp')), may hold values from -6 to 6
- cotangent: bfloat16 [16384, 1024], P(('fsdp', 'tp')), may hold values from -6 to 6
- qkv_weight: bfloat16 [1024, 3, 1024], P('fsdp', None, 'tp'), may hold values from -0.1875 to 0.1875
- qkv_bias: float32 [3, 1024], P(None, 'tp'), may hold values from -0.3 to 0.3
- out_weight: bfloat16 [1024, 1024], P('fsdp', 'tp'), may hold values from -1.5 to 1.5
- out_bias: float32 [1024], replicated, may hold values from -1.8 to 1.8
- up_weight: bfloat16 [1024, 4096], P('fsdp', 'tp'), may hold values from -0.1875 to 0.1875
- up_bias: float32 [4096], P('tp'), may hold values from -1.8 to 1.8
- down_weight: bfloat16 [1024, 4096], P('fsdp', 'tp'), may hold values from -0.09375 to 0.09375
- down_bias: float32 [1024], replicated, may hold values from -1.8 to 1.8
- attn_gain: float32 [1024], replicated, may hold values from 0.25 to 1.75
- attn_shift: float32 [1024], replicated, may hold values from -1.8 to 1.8
- mlp_gain: float32 [1024], replicated, may hold values from 0.25 to 1.75
- mlp_shift: float32 [1024], replicated, may hold values from -1.8 to 1.8
Outputs:
- mixed: bfloat16 [16384, 1024], P(('fsdp', 'tp'))
- tokens_grad: bfloat16 [16384, 1024], P(('fsdp', 'tp'))
- qkv_weight_grad: float32 [1024, 3, 1024], P('fsdp', None, 'tp')
- qkv_bias_grad: float32 [3, 1024], P(None, 'tp')
- out_weight_grad: float32 [1024, 1024], P('fsdp', 'tp')
- out_bias_grad: float32 [1024], replicated
- up_weight_grad: float32 [1024, 4096], P('fsdp', 'tp')
- up_bias_grad: float32 [4096], P('tp')
- down_weight_grad: float32 [1024, 4096], P('fsdp', 'tp')
- down_bias_grad: float32 [1024], replicated
- attn_gain_grad: float32 [1024], replicated
- attn_shift_grad: float32 [1024], replicated
- mlp_gain_grad: float32 [1024], replicated
- mlp_shift_grad: float32 [1024], replicated
All inputs are finite; a program needn't handle non-finite values.
Results may differ from a plain program's by a relative error of at most 0.014.
Values may be sent and summed in bfloat16 or wider, within the bound.
A program may use at most 192 MiB of HBM per device.

v0:
```python
import jax
import jax.numpy as jnp
from jax import lax
from jax.sharding import PartitionSpec as P

HD = 64
ROT = 16
SEQ = 1024


EPS = 1e-05
MASKED = -1e30
BASE = 10000.0
LAST = (((1,), (1,)), ((), ()))
FIRST = (((0,), (0,)), ((), ()))


def norm_rows(values):
    center = values - jnp.mean(values, axis=-1, keepdims=True)
    spread = jnp.mean(center * center, axis=-1, keepdims=True)
    factor = lax.rsqrt(spread + EPS)
    return (center * factor, factor)


def smooth(values):
    return jax.nn.gelu(values, approximate=False)


def rotary_tables(count):
    half = ROT // 2
    places = (jnp.arange(count, dtype=jnp.int32) % SEQ).astype(jnp.float32)
    rates = BASE ** (-2.0 * jnp.arange(half, dtype=jnp.float32) / ROT)
    angles = places[:, None] * rates[None, :]
    return (jnp.cos(angles)[:, None, :], jnp.sin(angles)[:, None, :])


def rotate(values, cosine, sine):
    half = ROT // 2
    first = values[..., :half]
    second = values[..., half:ROT]
    return jnp.concatenate(
        [first * cosine - second * sine, second * cosine + first * sine, values[..., ROT:]], axis=-1
    )


def causal_mask(part, block, end):
    places = part * block + jnp.arange(block, dtype=jnp.int32)
    return (jnp.arange(end, dtype=jnp.int32)[None, :] <= places[:, None])[None]


def block_scores(rows, key_seq, part, block, end, scale):
    scores = (
        jnp.einsum("qhd,khd->hqk", rows, key_seq[:end], preferred_element_type=jnp.float32) * scale
    )
    return jnp.where(causal_mask(part, block, end), scores, MASKED)


def attend_forward(queries, keys, values, scale):
    seqs = queries.shape[0] // SEQ
    block = min(512, SEQ)

    def one_sequence(index):
        outputs = []
        logs = []
        for part in range(SEQ // block):
            begin = part * block
            end = begin + block
            scores = block_scores(queries[begin:end], keys, part, block, end, scale)
            top = jnp.max(scores, axis=-1, keepdims=True)
            expo = jnp.exp(scores - top)
            total = jnp.sum(expo, axis=-1, keepdims=True)
            probs = (expo / total).astype(jnp.bfloat16)
            outputs.append(
                jnp.einsum("hqk,khd->qhd", probs, values[:end], preferred_element_type=jnp.float32)
            )
            logs.append(top[..., 0] + jnp.log(total[..., 0]))
        return (
            jnp.concatenate(outputs, axis=0).astype(jnp.bfloat16),
            jnp.concatenate(logs, axis=1),
        )

    return lax.map(one_sequence, jnp.arange(seqs, dtype=jnp.int32))


def attend_backward(queries, keys, values, grads, logsum, scale):
    seqs = queries.shape[0] // SEQ
    block = min(512, SEQ)

    def one_sequence(index):
        log_seq = lax.dynamic_index_in_dim(logsum, index, 0, keepdims=False)
        query_parts = []
        key_grad = jnp.zeros(keys.shape, jnp.float32)
        value_grad = jnp.zeros(values.shape, jnp.float32)
        for part in range(SEQ // block):
            begin = part * block
            end = begin + block
            rows = queries[begin:end]
            grad_block = grads[begin:end]
            scores = block_scores(rows, keys, part, block, end, scale)
            probs = jnp.exp(scores - log_seq[:, begin:end, None])
            prob_grad = jnp.einsum(
                "qhd,khd->hqk", grad_block, values[:end], preferred_element_type=jnp.float32
            )
            score_grad = (
                probs * (prob_grad - jnp.sum(probs * prob_grad, axis=-1, keepdims=True))
            ).astype(jnp.bfloat16)
            query_parts.append(
                jnp.einsum(
                    "hqk,khd->qhd", score_grad, keys[:end], preferred_element_type=jnp.float32
                )
                * scale
            )
            key_grad = key_grad.at[:end].add(
                jnp.einsum("hqk,qhd->khd", score_grad, rows, preferred_element_type=jnp.float32)
                * scale
            )
            value_grad = value_grad.at[:end].add(
                jnp.einsum(
                    "hqk,qhd->khd",
                    probs.astype(jnp.bfloat16),
                    grad_block,
                    preferred_element_type=jnp.float32,
                )
            )
        return (jnp.concatenate(query_parts, axis=0), key_grad, value_grad)

    return lax.map(one_sequence, jnp.arange(seqs, dtype=jnp.int32))


def local(
    tokens,
    cotangent,
    qkv_weight,
    qkv_bias,
    out_weight,
    out_bias,
    up_weight,
    up_bias,
    down_weight,
    down_bias,
    attn_gain,
    attn_shift,
    mlp_gain,
    mlp_shift,
):
    tp_count = lax.axis_size("tp")
    tp_index = lax.axis_index("tp")
    own_rows, width = tokens.shape
    cols = qkv_weight.shape[2]
    units = up_weight.shape[1]
    heads = cols // HD
    scale = HD ** (-0.5)
    all_tokens, grad_rows = (
        lax.all_gather(tokens, "tp", axis=0, tiled=True),
        lax.all_gather(cotangent, "tp", axis=0, tiled=True),
    )
    all_hat, all_factor = norm_rows(all_tokens.astype(jnp.float32))
    first_norm = (all_hat * attn_gain + attn_shift).astype(jnp.bfloat16)
    second_norm = (all_hat * mlp_gain + mlp_shift).astype(jnp.bfloat16)
    rows_all = first_norm.shape[0]
    flat_qkv = qkv_weight.reshape(qkv_weight.shape[0], 3 * cols)

    def keep_pieces():
        return ()

    output_store = ()
    pieces = (
        lax.all_gather(flat_qkv, "fsdp", axis=0, tiled=True),
        lax.all_gather(up_weight, "fsdp", axis=0, tiled=True),
    )
    qkv_sum = jnp.dot(first_norm, pieces[0], preferred_element_type=jnp.float32)
    up_sum = jnp.dot(second_norm, pieces[1], preferred_element_type=jnp.float32)
    inputs_done = (qkv_sum, up_sum) + keep_pieces()
    joined = inputs_done[0] + qkv_bias.reshape(3 * cols)
    up_pre = inputs_done[1] + up_bias
    cosine, sine = rotary_tables(rows_all)
    queries = rotate(joined[:, :cols].reshape(rows_all, heads, HD), cosine, sine).astype(
        jnp.bfloat16
    )
    keys = rotate(joined[:, cols : 2 * cols].reshape(rows_all, heads, HD), cosine, sine).astype(
        jnp.bfloat16
    )
    values = joined[:, 2 * cols :].reshape(rows_all, heads, HD).astype(jnp.bfloat16)
    attended, logsum = attend_forward(queries, keys, values, scale)
    attended = attended.reshape(rows_all, cols)
    activated = smooth(up_pre).astype(jnp.bfloat16)
    outputs_init = (jnp.zeros((rows_all, width), jnp.float32),) + output_store
    pieces = (
        lax.all_gather(out_weight, "fsdp", axis=0, tiled=True),
        lax.all_gather(down_weight, "fsdp", axis=0, tiled=True),
    )
    block = lax.dot_general(attended, pieces[0], LAST, preferred_element_type=jnp.float32)
    block = block + lax.dot_general(activated, pieces[1], LAST, preferred_element_type=jnp.float32)
    outputs_done = (
        lax.dynamic_update_slice_in_dim(outputs_init[0], block, jnp.int32(0), 1),
    ) + keep_pieces()
    branch = lax.psum_scatter(outputs_done[0], "tp", scatter_dimension=0, tiled=True)
    mixed = (tokens.astype(jnp.float32) + branch + (out_bias + down_bias)).astype(jnp.bfloat16)
    pieces = (
        lax.all_gather(out_weight, "fsdp", axis=0, tiled=True),
        lax.all_gather(down_weight, "fsdp", axis=0, tiled=True),
    )
    left = grad_rows
    att_grad = jnp.dot(left, pieces[0], preferred_element_type=jnp.float32)
    act_grad = jnp.dot(left, pieces[1], preferred_element_type=jnp.float32)
    att_grad16 = att_grad.astype(jnp.bfloat16)
    pre_grad16 = jax.vjp(smooth, up_pre)[1](act_grad)[0].astype(jnp.bfloat16)
    query_grad, key_grad, value_grad = attend_backward(
        queries, keys, values, att_grad16.reshape(rows_all, heads, HD), logsum, scale
    )
    query_grad = rotate(query_grad.reshape(rows_all, heads, HD), cosine, -sine)
    key_grad = rotate(key_grad.reshape(rows_all, heads, HD), cosine, -sine)
    joined_grad = jnp.concatenate(
        [
            query_grad.reshape(rows_all, cols),
            key_grad.reshape(rows_all, cols),
            value_grad.reshape(rows_all, cols),
        ],
        axis=1,
    ).astype(jnp.bfloat16)
    shard_rows = qkv_weight.shape[0]

    def cross(left, right):
        return lax.dot_general(left, right, FIRST, preferred_element_type=jnp.float32)

    weight_sums = lax.psum_scatter(
        jnp.concatenate(
            [
                cross(first_norm, joined_grad),
                cross(grad_rows, attended),
                cross(second_norm, pre_grad16),
                cross(grad_rows, activated),
            ],
            axis=1,
        ).astype(jnp.bfloat16),
        "fsdp",
        scatter_dimension=0,
        tiled=True,
    ).astype(jnp.float32)
    qkv_weight_grad = weight_sums[:, : 3 * cols].reshape(shard_rows, 3, cols)
    out_weight_grad = weight_sums[:, 3 * cols : 4 * cols]
    up_weight_grad = weight_sums[:, 4 * cols : 4 * cols + units]
    down_weight_grad = weight_sums[:, 4 * cols + units :]
    pieces = (
        lax.all_gather(flat_qkv, "fsdp", axis=0, tiled=True),
        lax.all_gather(up_weight, "fsdp", axis=0, tiled=True),
    )
    first_block = lax.dot_general(joined_grad, pieces[0], LAST, preferred_element_type=jnp.float32)
    second_block = lax.dot_general(pre_grad16, pieces[1], LAST, preferred_element_type=jnp.float32)
    grad_own = cotangent.astype(jnp.float32)
    gain_terms = jnp.stack(
        [
            jnp.sum(first_block * all_hat, axis=0),
            jnp.sum(first_block, axis=0),
            jnp.sum(second_block * all_hat, axis=0),
            jnp.sum(second_block, axis=0),
            jnp.sum(grad_own, axis=0),
        ]
    )
    hat_grad = lax.psum_scatter(
        first_block * attn_gain + second_block * mlp_gain, "tp", scatter_dimension=0, tiled=True
    )
    hat_own = lax.dynamic_slice_in_dim(all_hat, tp_index * own_rows, own_rows, 0)
    factor_own = lax.dynamic_slice_in_dim(all_factor, tp_index * own_rows, own_rows, 0)
    center_grad = (
        hat_grad
        - jnp.mean(hat_grad, axis=-1, keepdims=True)
        - hat_own * jnp.mean(hat_grad * hat_own, axis=-1, keepdims=True)
    )
    tokens_grad = (grad_own + factor_own * center_grad).astype(jnp.bfloat16)
    qkv_bias_own = jnp.sum(joined_grad, axis=0, dtype=jnp.float32).reshape(3, cols)
    up_bias_own = jnp.sum(pre_grad16, axis=0, dtype=jnp.float32)
    qkv_spread = lax.dynamic_update_slice_in_dim(
        jnp.zeros((3, width), jnp.float32), qkv_bias_own, tp_index * cols, 1
    )
    up_spread = lax.dynamic_update_slice_in_dim(
        jnp.zeros((units * tp_count,), jnp.float32), up_bias_own, tp_index * units, 0
    )
    gain_total, qkv_total, up_total = lax.psum((gain_terms, qkv_spread, up_spread), ("fsdp", "tp"))
    qkv_bias_grad = lax.dynamic_slice_in_dim(qkv_total, tp_index * cols, cols, 1)
    up_bias_grad = lax.dynamic_slice_in_dim(up_total, tp_index * units, units, 0)
    return (
        mixed,
        tokens_grad,
        qkv_weight_grad,
        qkv_bias_grad,
        out_weight_grad,
        gain_total[4],
        up_weight_grad,
        up_bias_grad,
        down_weight_grad,
        gain_total[4],
        gain_total[0],
        gain_total[1],
        gain_total[2],
        gain_total[3],
    )


def solution(mesh):
    return jax.shard_map(
        local,
        mesh=mesh,
        in_specs=(
            P(("fsdp", "tp"), None),
            P(("fsdp", "tp"), None),
            P("fsdp", None, "tp"),
            P(None, "tp"),
            P("fsdp", "tp"),
            P(),
            P("fsdp", "tp"),
            P("tp"),
            P("fsdp", "tp"),
            P(),
            P(),
            P(),
            P(),
            P(),
        ),
        out_specs=(
            P(("fsdp", "tp"), None),
            P(("fsdp", "tp"), None),
            P("fsdp", None, "tp"),
            P(None, "tp"),
            P("fsdp", "tp"),
            P(),
            P("fsdp", "tp"),
            P("tp"),
            P("fsdp", "tp"),
            P(),
            P(),
            P(),
            P(),
            P(),
        ),
        check_vma=False,
    )
```

profile of v0, /device:TPU:0, one launch (start us, length us, event | category | flops | bytes accessed | tf_op | source)
XLA Modules:
  0.0 588.8 jit_solution(10351848363227599973)
XLA Ops:
  9.4 1.6 copy.63
  13.8 1.2 iota_compare_fusion
  15.8 29.6 %all-gather.7.cloned.1.call-done = bf16[1024,1024]{1,0:T(8,128)(2,1)} async-done(((bf16[512,1024]{1,0:T(8,128)(2,1)}), bf16[1024,1024]{1,0:T(8,128)(2,1)}) %all-gather.7.cloned.1.call-update) | async-done | bytes 2097168 | tf_op jit(solution)/shard_map/all_gather | solution.py:154
  45.4 1.9 convert_reduce_fusion.2
  47.3 2.3 fusion.16
  49.7 35.9 %all-gather.11.cloned.1.call-done = bf16[1024,512]{1,0:T(8,128)(2,1)} async-done(((bf16[64,512]{1,0:T(8,128)(2,1)}), bf16[1024,512]{1,0:T(8,128)(2,1)}) %all-gather.11.cloned.1.call-update) | async-done | bytes 1048592 | tf_op jit(solution)/shard_map/all_gather | solution.py:189
  85.5 33.6 %all-gather.17.cloned.1.call-done = bf16[1024,1024]{1,0:T(8,128)(2,1)} async-done(((bf16[512,1024]{1,0:T(8,128)(2,1)}), bf16[1024,1024]{1,0:T(8,128)(2,1)}) %all-gather.17.cloned.1.call-update) | async-done | bytes 2097168 | tf_op jit(solution)/shard_map/all_gather | solution.py:155
  119.2 3.1 convolution_convert_fusion.3
  122.3 0.9 fusion.57
  123.2 43.9 %all-gather.9.cloned.1.call-done = bf16[1024,1536]{1,0:T(8,128)(2,1)} async-done(((bf16[64,1536]{1,0:T(8,128)(2,1)}), bf16[1024,1536]{1,0:T(8,128)(2,1)}) %all-gather.9.cloned.1.call-update) | async-done | bytes 3145744 | tf_op jit(solution)/shard_map/all_gather | solution.py:168
  167.1 5.5 fusion.60
  172.6 0.8 slice.256
  173.4 1.0 slice.266
  174.5 2.5 fusion.56
  177.0 3.1 copy.47
  180.1 2.9 copy.48
  183.0 1.6 slice.339
  184.6 1.5 slice.338
  186.1 1.6 subtract_convert_fusion.2
  187.9 1.6 fusion.62
  189.5 1.2 fusion.12
  190.7 2.1 copy-done.2
  193.4 2.1 copy.46
  195.4 4.5 fusion.61
  200.0 3.8 fusion
  203.8 1.9 copy-done
  206.1 2.3 copy.50
  208.4 10.5 %multiply_reduce_fusion.1 = (f32[8,512]{1,0:T(8,128)}, f32[8,512,512]{1,2,0:T(8,128)}) fusion(f32[8,512,512]{1,2,0:T(8,128)} %copy-done.2, f32[8,512]{1,0:T(8,128)} %log_add_fusion.1, bf16[512,8,64]{0,2,1:T(8,128)(2,1)} %bitcast.83, bf16[512,8,64]{0,2,1:T(8,128)(2,1)} %bitcast.96), kind=kOutput, calls=%fused_computation.16 | convolution fusion | flops 274722816 | bytes 17858560 | tf_op jit(solution)/shard_map/while/body/eval_jaxpr/qhd,khd->hqk/dot_general | solution.py:101
  218.9 1.2 copy-done.1
  220.1 10.1 %multiply_reduce_fusion = (f32[8,512]{1,0:T(8,128)}, f32[8,512,1024]{2,1,0:T(8,128)}) fusion(f32[8,512,1024]{2,1,0:T(8,128)S(1)} %copy-done.1, f32[8,512]{1,0:T(8,128)S(1)} %log_add_fusion, bf16[512,8,64]{0,2,1:T(8,128)(2,1)S(1)} %bitcast.81, bf16[1024,8,64]{0,2,1:T(8,128)(2,1)} %bitcast.88), kind=kOutput, calls=%fused_computation.1 | convolution fusion | flops 549449728 | bytes 35160064 | tf_op jit(solution)/shard_map/while/body/eval_jaxpr/qhd,khd->hqk/dot_general | solution.py:101
  230.2 7.1 %multiply_convert_fusion.1 = bf16[8,512,512]{1,2,0:T(8,128)(2,1)S(1)} fusion(f32[8,512,512]{1,2,0:T(8,128)} %get-tuple-element.222, f32[8,512,512]{1,2,0:T(8,128)} %copy-done.2, f32[8,512]{1,0:T(8,128)} %get-tuple-element.221, f32[8,512]{1,0:T(8,128)} %log_add_fusion.1), kind=kLoop, calls=%fused_computation.15 | loop fusion | flops 8388608 | bytes 21004288 | tf_op jit(solution)/shard_map/while/body/eval_jaxpr/convert_element_type | solution.py:106
  237.4 2.4 fusion.30
  239.8 8.1 %multiply_convert_fusion = bf16[8,512,1024]{2,1,0:T(8,128)(2,1)S(1)} fusion(f32[8,512,1024]{2,1,0:T(8,128)} %get-tuple-element.224, f32[8,512,1024]{2,1,0:T(8,128)S(1)} %copy-done.1, f32[8,512]{1,0:T(8,128)S(1)} %copy-done.37, f32[8,512]{1,0:T(8,128)S(1)} %log_add_fusion), kind=kLoop, calls=%fused_computation | loop fusion | flops 16777216 | bytes 41975808 | tf_op jit(solution)/shard_map/while/body/eval_jaxpr/convert_element_type | solution.py:106
  247.9 4.4 bitcast_add_fusion.1
  252.3 1.0 slice.337
  255.3 6.1 %fusion.32 = f32[512,8,64]{0,2,1:T(8,128)S(1)} fusion(bf16[8,512,1024]{2,1,0:T(8,128)(2,1)} %copy-done.3, bf16[1024,8,48]{0,2,1:T(8,128)(2,1)S(1)} %copy-done.10, bf16[1024,8,8]{0,2,1:T(8,128)(2,1)S(1)} %copy-done.30, bf16[1024,8,8]{0,2,1:T(8,128)(2,1)S(1)} %copy-done.28), kind=kOutput, calls=%fused_computation.85 | convolution fusion | flops 540278784 | bytes 10485760 | tf_op jit(solution)/shard_map/while/body/eval_jaxpr/hqk,khd->qhd/dot_general | solution.py:108
  261.7 0.8 copy-done.25
  262.5 1.2 pad_maximum_fusion.6
  263.7 5.3 fusion.27
  269.1 3.0 fusion.22
  272.1 0.9 copy-done.15
  273.1 7.0 %fusion.50 = f32[1024,1024]{1,0:T(8,128)} fusion(bf16[1024,1536]{1,0:T(8,128)(2,1)} %all-gather.9.cloned.1.call-done, bf16[1024,512]{0,1:T(8,128)(2,1)S(1)} %bitcast.85, bf16[1024,512]{0,1:T(8,128)(2,1)S(1)} %bitcast.94, bf16[1024,512]{0,1:T(8,128)(2,1)S(1)} %bitcast.90), kind=kOutput, calls=%fused_computation.133 | convolution fusion | flops 3230662656 | bytes 10485760 | tf_op jit(solution)/shard_map/dot_general | solution.py:248
  280.1 9.6 %fusion.51 = f32[1024,2048]{1,0:T(8,128)} fusion(bf16[1024,2048]{1,0:T(8,128)(2,1)} %all-gather.13.cloned.1.call-done, bf16[1024,1024]{1,0:T(8,128)(2,1)S(1)} %copy-done.7, f32[1024]{0:T(1024)S(1)} %copy-done.61, f32[1024]{0:T(1024)S(1)} %copy-done.60, f32[1024]{0:T(1024)S(1)} %add_rsqrt_fusion, f32[1024]{0:T(1024)S(1)} %broadcast_multiply_fusion), kind=kOutput, calls=%fused_computation.134 | convolution fusion | flops 4301258752 | bytes 14696448 | tf_op jit(solution)/shard_map/dot_general | solution.py:172
  289.7 27.7 %convert_reduce_fusion = (f32[2048]{0:T(1024)S(1)}, bf16[1024,2048]{1,0:T(8,128)(2,1)S(1)}, f32[1024,2048]{1,0:T(8,128)}) fusion(f32[1024,2048]{1,0:T(8,128)} %fusion.51, f32[2048]{0:T(1024)S(1)} %copy-done.47, bf16[1024,1024]{1,0:T(8,128)(2,1)} %all-gather.17.cloned.1.call-done, bf16[1024,2048]{1,0:T(8,128)(2,1)} %all-gather.15.cloned.1.call-done), kind=kOutput, calls=%fused_computation.12 | convolution fusion | flops 4452251648 | bytes 27279360 | tf_op jit(solution)/shard_map/dot_general | solution.py:205
  317.4 8.6 %fusion.52 = (f32[1024]{0:T(1024)}, f32[1024]{0:T(1024)}, f32[1024,1024]{1,0:T(8,128)}, f32[1024]{0:T(1024)}, f32[1024]{0:T(1024)}, /*index=5*/f32[1024,1024]{1,0:T(8,128)}) fusion(f32[1024]{0:T(1024)S(1)} %add_rsqrt_fusion, f32[1024]{0:T(1024)S(1)} %broadcast_multiply_fusion, bf16[1024,1024]{1,0:T(8,128)(2,1)S(1)} %copy-done.7, f32[1024]{0:T(1024)S(1)} %copy-done.60, ...), kind=kOutput, calls=%fused_computation.135 | convolution fusion | flops 4307546112 | bytes 23101440 | tf_op jit(solution)/shard_map/dot_general | solution.py:249
  327.1 5.0 fusion.33
  332.1 7.5 %fusion.34 = bf16[8,64,512]{2,1,0:T(8,128)(2,1)S(1)} fusion(bf16[1024,8,64]{0,2,1:T(8,128)(2,1)S(1)} %bitcast.89, f32[8,512,1024]{2,1,0:T(8,128)} %copy-done, f32[8,512]{1,0:T(8,128)S(1)} %copy-done.45, f32[8,512]{1,0:T(8,128)S(1)} %copy-done.43), kind=kOutput, calls=%fused_computation.87 | convolution fusion | flops 549715968 | bytes 18382848 | tf_op jit(solution)/shard_map/while/body/eval_jaxpr/hqk,khd->qhd/dot_general | solution.py:74
  339.6 10.2 %multiply_convert_fusion.2 = bf16[1024,2048]{1,0:T(8,128)(2,1)} fusion(f32[1024,2048]{1,0:T(8,128)} %get-tuple-element.182, f32[1024,2048]{1,0:T(8,128)} %fusion.51, f32[2048]{0:T(1024)S(1)} %copy-done.47), kind=kLoop, calls=%fused_computation.18 | loop fusion | flops 8388608 | bytes 20979712 | tf_op jit(solution)/shard_map/convert_element_type | solution.py:186
  349.8 7.9 %fusion.63 = f32[1024,1024]{1,0:T(8,128)S(1)} fusion(bf16[1024,2048]{1,0:T(8,128)(2,1)} %multiply_convert_fusion.2, bf16[1024,2048]{1,0:T(8,128)(2,1)} %all-gather.15.cloned.1.call-done), kind=kOutput, calls=%fused_computation.145 | convolution fusion | flops 4294967296 | bytes 12582912 | tf_op jit(solution)/shard_map/dot_general | solution.py:193
  357.8 3.4 convolution_add_fusion.1
  361.5 3.9 fusion.26
  365.4 2.3 copy.55
  367.7 6.1 %convolution_convert_fusion = bf16[1024,1536]{1,0:T(8,128)(2,1)S(1)} fusion(bf16[1024,512]{0,1:T(8,128)(2,1)} %bitcast.86, bf16[1024,512]{0,1:T(8,128)(2,1)} %bitcast.93, bf16[1024,512]{0,1:T(8,128)(2,1)} %bitcast.91, bf16[1024,1024]{1,0:T(8,128)(2,1)S(1)} %copy-done.7, f32[1024]{0:T(1024)S(1)} %copy-done.57, f32[1024]{0:T(1024)S(1)} %copy-done.59, ...), kind=kOutput, calls=%fused_computation.54 | convolution fusion | flops 3238526976 | bytes 8404992 | tf_op jit(solution)/shard_map/dot_general | solution.py:224
  373.8 5.0 convert_bitcast_fusion
  378.9 5.5 convolution_convert_fusion.1
  384.4 10.4 %pad_maximum_fusion = bf16[1024,6144]{1,0:T(8,128)(2,1)} fusion(bf16[1024,2048]{1,0:T(8,128)(2,1)S(1)} %convert_bitcast_fusion, bf16[1024,2048]{1,0:T(8,128)(2,1)S(1)} %convolution_convert_fusion.1, bf16[1024,512]{1,0:T(8,128)(2,1)S(1)} %copy-done.19, bf16[1024,1536]{1,0:T(8,128)(2,1)S(1)} %convolution_convert_fusion), kind=kLoop, calls=%fused_computation.8 | loop fusion | flops 50331648 | bytes 25165824 | tf_op jit(solution)/shard_map/concatenate | solution.py:227
  398.0 2.8 fusion.54
  400.9 3.3 convert_reduce_fusion.3
  404.2 40.7 %all-reduce.2 = (f32[3,1024]{1,0:T(4,128)S(1)}, f32[5,1024]{1,0:T(8,128)S(1)}, f32[4096]{0:T(1024)S(1)}) all-reduce(f32[3,1024]{1,0:T(4,128)S(1)} %constant_dynamic-update-slice_fusion, f32[5,1024]{1,0:T(8,128)S(1)} %stack.23, f32[4096]{0:T(1024)S(1)} %dynamic_update_slice.20), channel_id=1, replica_groups=mesh['fsdp'=16,'tp'=2] {'fsdp','tp'}, use_global_device_ids=true, to_apply=%region_14.15 | all-reduce | flops 12288 | bytes 98304 | tf_op jit(solution)/shard_map/psum | solution.py:279
  446.7 2.9 add_convert_fusion.3
  449.7 126.1 %reduce-scatter.8.cloned.1.call-done = bf16[64,6144]{1,0:T(8,128)(2,1)} async-done(((bf16[1024,6144]{1,0:T(8,128)(2,1)}), bf16[64,6144]{1,0:T(8,128)(2,1)}) %reduce-scatter.8.cloned.1.call-update) | async-done | bytes 786448 | tf_op jit(solution)/shard_map/reduce_scatter | solution.py:226
  575.8 1.0 slice.277
  577.5 2.1 fusion.58
  579.6 1.5 slice.278
  (177 shorter events, 16.9 us)
Async XLA Ops:
  7.2 38.2 %all-gather.7.cloned.1.call-start = ((), (), s32[]{:S(2)}) async-start(), calls=%async_computation.3 | async-start | bytes 3145728 | tf_op jit(solution)/shard_map/all_gather | solution.py:154
  7.9 77.6 %all-gather.11.cloned.1.call-start = ((), (), s32[]{:S(2)}) async-start(), calls=%async_computation.5 | async-start | bytes 1114112 | tf_op jit(solution)/shard_map/all_gather | solution.py:189
  8.7 110.5 %all-gather.17.cloned.1.call-start = ((), (), s32[]{:S(2)}) async-start(), calls=%async_computation.9 | async-start | bytes 3145728 | tf_op jit(solution)/shard_map/all_gather | solution.py:155
  9.4 157.7 %all-gather.9.cloned.1.call-start = ((), (), s32[]{:S(2)}) async-start(), calls=%async_computation.4 | async-start | bytes 3342336 | tf_op jit(solution)/shard_map/all_gather | solution.py:168
  11.1 269.0 %all-gather.13.cloned.1.call-start = ((), (), s32[]{:S(2)}) async-start(), calls=%async_computation.6 | async-start | bytes 4456448 | tf_op jit(solution)/shard_map/all_gather | solution.py:169
  11.7 278.0 %all-gather.15.cloned.1.call-start = ((), (), s32[]{:S(2)}) async-start(), calls=%async_computation.7 | async-start | bytes 4456448 | tf_op jit(solution)/shard_map/all_gather | solution.py:190
  12.3 385.7 %reduce-scatter.6.cloned.1.call-start = ((), (), s32[]{:S(2)}) async-start(), calls=%async_computation.10 | async-start | bytes 6291456 | tf_op jit(solution)/shard_map/reduce_scatter | solution.py:260
  15.8 170.4 %copy-start.32 = (f32[1024,8]{0,1:T(8,128)}, f32[1024,8]{0,1:T(8,128)S(1)}, u32[]{:S(2)}) copy-start(f32[1024,8]{0,1:T(8,128)S(1)} %get-tuple-element.214) | copy-start | bytes 98308
  49.6 117.5 %copy-start.7 = (bf16[1024,1024]{1,0:T(8,128)(2,1)S(1)}, bf16[1024,1024]{1,0:T(8,128)(2,1)}, u32[]{:S(2)}) copy-start(bf16[1024,1024]{1,0:T(8,128)(2,1)} %all-gather.7.cloned.1.call-done) | copy-start | bytes 6291460
  49.6 117.5 %copy-start.56 = (f32[1024]{0:T(1024)S(1)}, f32[1024]{0:T(1024)}, u32[]{:S(2)}) copy-start(f32[1024]{0:T(1024)} %param.37) | copy-start | bytes 12292
  49.7 117.4 %copy-start.58 = (f32[1024]{0:T(1024)S(1)}, f32[1024]{0:T(1024)}, u32[]{:S(2)}) copy-start(f32[1024]{0:T(1024)} %param.36) | copy-start | bytes 12292
  183.0 4.9 copy-start.34
  186.1 9.3 %copy-start.8 = (bf16[1024,8,48]{0,2,1:T(8,128)(2,1)}, bf16[1024,8,48]{0,2,1:T(8,128)(2,1)S(1)}, u32[]{:S(2)}) copy-start(bf16[1024,8,48]{0,2,1:T(8,128)(2,1)S(1)} %slice.338) | copy-start | bytes 2359300
  187.7 1.7 copy-start.27
  187.8 1.7 copy-start.29
  187.8 1.6 copy-start.11
  189.5 3.3 copy-start.2
  189.5 3.3 copy-start.38
  192.8 7.2 %copy-start.40 = (f32[8,512]{1,0:T(8,128)}, f32[8,512]{1,0:T(8,128)S(1)}, u32[]{:S(2)}) copy-start(f32[8,512]{1,0:T(8,128)S(1)} %fusion.12) | copy-start | bytes 49156
  200.0 5.8 copy-start
  200.0 6.1 %copy-start.42 = (f32[8,512]{1,0:T(8,128)}, f32[8,512]{1,0:T(8,128)S(1)}, u32[]{:S(2)}) copy-start(f32[8,512]{1,0:T(8,128)S(1)} %get-tuple-element.217) | copy-start | bytes 49156
  206.1 2.3 copy-start.44
  208.4 11.7 %copy-start.1 = (f32[8,512,1024]{2,1,0:T(8,128)S(1)}, f32[8,512,1024]{2,1,0:T(8,128)}, u32[]{:S(2)}) copy-start(f32[8,512,1024]{2,1,0:T(8,128)} %copy-done) | copy-start | bytes 50331652
  230.2 7.1 %copy-start.12 = (bf16[1024,8,64]{0,2,1:T(8,128)(2,1)S(1)}, bf16[1024,8,64]{0,2,1:T(8,128)(2,1)}, u32[]{:S(2)}) copy-start(bf16[1024,8,64]{0,2,1:T(8,128)(2,1)} %copy-done.11) | copy-start | bytes 3145732
  237.4 2.4 copy-start.4
  237.4 2.4 copy-start.37
  247.9 4.5 copy-start.3
  247.9 6.0 %copy-start.5 = (bf16[8,512,512]{1,2,0:T(8,128)(2,1)S(1)}, bf16[8,512,512]{1,2,0:T(8,128)(2,1)}, u32[]{:S(2)}) copy-start(bf16[8,512,512]{1,2,0:T(8,128)(2,1)} %copy-done.4) | copy-start | bytes 12582916
  247.9 6.2 %copy-start.9 = (bf16[1024,8,48]{0,2,1:T(8,128)(2,1)S(1)}, bf16[1024,8,48]{0,2,1:T(8,128)(2,1)}, u32[]{:S(2)}) copy-start(bf16[1024,8,48]{0,2,1:T(8,128)(2,1)} %copy-done.8) | copy-start | bytes 2359300
  247.9 6.2 %copy-start.28 = (bf16[1024,8,8]{0,2,1:T(8,128)(2,1)S(1)}, bf16[1024,8,8]{0,2,1:T(8,128)(2,1)}, u32[]{:S(2)}) copy-start(bf16[1024,8,8]{0,2,1:T(8,128)(2,1)} %copy-done.27) | copy-start | bytes 393220
  247.9 6.2 %copy-start.30 = (bf16[1024,8,8]{0,2,1:T(8,128)(2,1)S(1)}, bf16[1024,8,8]{0,2,1:T(8,128)(2,1)}, u32[]{:S(2)}) copy-start(bf16[1024,8,8]{0,2,1:T(8,128)(2,1)} %copy-done.29) | copy-start | bytes 393220
  255.3 6.2 %copy-start.33 = (f32[1024,8]{0,1:T(8,128)S(1)}, f32[1024,8]{0,1:T(8,128)}, u32[]{:S(2)}) copy-start(f32[1024,8]{0,1:T(8,128)} %copy-done.32) | copy-start | bytes 98308
  255.3 6.3 %copy-start.36 = (f32[1024,8]{0,1:T(8,128)S(1)}, f32[1024,8]{0,1:T(8,128)}, u32[]{:S(2)}) copy-start(f32[1024,8]{0,1:T(8,128)} %get-tuple-element.212) | copy-start | bytes 98308
  261.5 2.2 copy-start.13
  261.5 2.2 copy-start.35
  263.7 8.4 %copy-start.20 = (bf16[1024,8,64]{0,2,1:T(8,128)(2,1)}, bf16[1024,8,64]{0,2,1:T(8,128)(2,1)S(1)}, u32[]{:S(2)}) copy-start(bf16[1024,8,64]{0,2,1:T(8,128)(2,1)S(1)} %get-tuple-element.225) | copy-start | bytes 3145732
  269.1 4.0 copy-start.22
  273.1 7.0 %copy-start.60 = (f32[1024]{0:T(1024)S(1)}, f32[1024]{0:T(1024)}, u32[]{:S(2)}) copy-start(f32[1024]{0:T(1024)} %param.38) | copy-start | bytes 12292
  273.1 7.0 %copy-start.61 = (f32[1024]{0:T(1024)S(1)}, f32[1024]{0:T(1024)}, u32[]{:S(2)}) copy-start(f32[1024]{0:T(1024)} %param.39) | copy-start | bytes 12292
  280.1 9.6 %copy-start.47 = (f32[2048]{0:T(1024)S(1)}, f32[2048]{0:T(1024)}, u32[]{:S(2)}) copy-start(f32[2048]{0:T(1024)} %param.33) | copy-start | bytes 24580
  289.7 27.8 %copy-start.59 = (f32[1024]{0:T(1024)S(1)}, f32[1024]{0:T(1024)}, u32[]{:S(2)}) copy-start(f32[1024]{0:T(1024)} %param.36) | copy-start | bytes 12292
  289.7 27.8 %copy-start.54 = (bf16[1024,2048]{1,0:T(8,128)(2,1)S(1)}, bf16[1024,2048]{1,0:T(8,128)(2,1)}, u32[]{:S(2)}) copy-start(bf16[1024,2048]{1,0:T(8,128)(2,1)} %all-gather.13.cloned.1.call-done) | copy-start | bytes 12582916
  289.7 27.8 %copy-start.62 = (f32[1024,1024]{1,0:T(8,128)S(1)}, f32[1024,1024]{1,0:T(8,128)}, u32[]{:S(2)}) copy-start(f32[1024,1024]{1,0:T(8,128)} %fusion.50) | copy-start | bytes 12582916
  317.4 8.6 %copy-start.63 = (bf16[1024,2048]{1,0:T(8,128)(2,1)}, bf16[1024,2048]{1,0:T(8,128)(2,1)S(1)}, u32[]{:S(2)}) copy-start(bf16[1024,2048]{1,0:T(8,128)(2,1)S(1)} %get-tuple-element.181) | copy-start | bytes 12582916
  326.1 6.0 %copy-start.43 = (f32[8,512]{1,0:T(8,128)S(1)}, f32[8,512]{1,0:T(8,128)}, u32[]{:S(2)}) copy-start(f32[8,512]{1,0:T(8,128)} %copy-done.42) | copy-start | bytes 49156
  326.1 6.0 %copy-start.45 = (f32[8,512]{1,0:T(8,128)S(1)}, f32[8,512]{1,0:T(8,128)}, u32[]{:S(2)}) copy-start(f32[8,512]{1,0:T(8,128)} %copy-done.44) | copy-start | bytes 49156
  326.1 120.6 %reduce-scatter.4.cloned.1.call-start = ((), (), s32[]{:S(2)}) async-start(), calls=%async_computation.8 | async-start | bytes 6291456 | tf_op jit(solution)/shard_map/reduce_scatter | solution.py:197
  327.1 5.0 copy-start.18
  349.8 7.9 %copy-start.31 = (bf16[1024,512]{1,0:T(8,128)(2,1)S(1)}, bf16[1024,512]{1,0:T(8,128)(2,1)}, u32[]{:S(2)}) copy-start(bf16[1024,512]{1,0:T(8,128)(2,1)} %all-gather.11.cloned.1.call-done) | copy-start | bytes 3145732
  361.2 6.5 %copy-start.57 = (f32[1024]{0:T(1024)S(1)}, f32[1024]{0:T(1024)}, u32[]{:S(2)}) copy-start(f32[1024]{0:T(1024)} %param.37) | copy-start | bytes 12292
  361.2 214.6 %reduce-scatter.8.cloned.1.call-start = ((), (), s32[]{:S(2)}) async-start(), calls=%async_computation.11 | async-start | bytes 13369344 | tf_op jit(solution)/shard_map/reduce_scatter | solution.py:226
  367.7 6.1 %copy-start.14 = (bf16[1024,2048]{1,0:T(8,128)(2,1)S(1)}, bf16[1024,2048]{1,0:T(8,128)(2,1)}, u32[]{:S(2)}) copy-start(bf16[1024,2048]{1,0:T(8,128)(2,1)} %multiply_convert_fusion.2) | copy-start | bytes 12582916
  367.7 6.1 %copy-start.55 = (bf16[1024,1024]{1,0:T(8,128)(2,1)S(1)}, bf16[1024,1024]{1,0:T(8,128)(2,1)}, u32[]{:S(2)}) copy-start(bf16[1024,1024]{1,0:T(8,128)(2,1)} %all-gather.17.cloned.1.call-done) | copy-start | bytes 6291460
  373.8 5.1 copy-start.64
  378.8 5.5 copy-start.19
  394.8 1.9 copy-start.23
  397.3 3.5 copy-start.24
  398.0 2.9 copy-start.6
  400.7 3.5 copy-start.50
  400.7 3.4 copy-start.51
  400.7 3.4 copy-start.52
  400.8 3.4 copy-start.53
  400.8 46.0 %copy-start.17 = (bf16[512,1024]{1,0:T(8,128)(2,1)S(1)}, bf16[512,1024]{1,0:T(8,128)(2,1)}, u32[]{:S(2)}) copy-start(bf16[512,1024]{1,0:T(8,128)(2,1)} %param.26) | copy-start | bytes 3145732
  445.5 136.2 %copy-start.46 = (f32[1,1024]{1,0:T(1,128)}, f32[1,1024]{1,0:T(1,128)S(1)}, u32[]{:S(2)}) copy-start(f32[1,1024]{1,0:T(1,128)S(1)} %get-tuple-element.211) | copy-start | bytes 12292
  (10 other events, 10.6 us)
Sparse Core Ops, SparseCore 0:
  9.6 35.7 all-gather.6
  47.6 37.9 all-gather.10
  87.1 32.0 all-gather.16
  121.9 45.1 all-gather.8
  169.1 49.3 all-gather.12
  220.5 49.0 all-gather.14
  326.2 53.2 reduce-scatter.5
  381.8 55.0 reduce-scatter.3
  441.0 134.7 reduce-scatter.7
where the time goes:
time: 595 us; the launch traced here: 589 us
  waiting for transfers between devices  272 us (46%)
  matrix products  155 us (26%)
  other arithmetic  61.1 us (10%)
  local copies, waits for them, and re-layouts  44.1 us (7%)
  blocking collectives  40.7 us (7%)
  between operations  15.2 us (3%)
    reduce_scatter x1, waiting for transfers between devices, local(): lax.psum_scatter(jnp.concatenate([cross(first_norm, joined_grad), cross(g...  126 us
    all_gather x1, waiting for transfers between devices, local(): lax.all_gather(flat_qkv, 'fsdp', axis=0, tiled=True)  43.9 us
    psum x1, blocking collectives, local(): lax.psum((gain_terms, qkv_spread, up_spread), ('fsdp', 'tp'))  40.7 us
    all_gather x1, waiting for transfers between devices, local(): lax.all_gather(out_weight, 'fsdp', axis=0, tiled=True)  35.9 us
    all_gather x1, waiting for transfers between devices, local(): lax.all_gather(cotangent, 'tp', axis=0, tiled=True)  33.6 us
    all_gather x1, waiting for transfers between devices, local(): lax.all_gather(tokens, 'tp', axis=0, tiled=True)  29.6 us
    dot_general x1, matrix products, local(): act_grad = jnp.dot(left, pieces[1], preferred_element_type=jnp.float32)  27.7 us
    dot_general x2, matrix products, one_sequence(): jnp.einsum('qhd,khd->hqk', grad_block, values[:end], preferred_element_ty...  20.6 us
  transfers between devices with their start and end apart: 9, of which 5 were waited for; matrix products, arithmetic and copies ran while one was open for 35% of the time, Pallas kernels for 0%

commit v1 on v0

v1 whole, which is shorter than its diff:
```python
import functools

import jax
import jax.numpy as jnp
import numpy as np
from jax import lax
from jax.experimental import pallas as pl
from jax.experimental.pallas import tpu as pltpu
from jax.sharding import PartitionSpec as P

HD = 64
ROT = 16
SEQ = 1024
QBLOCK = 256


EPS = 1e-05
MASKED = -1e30
BASE = 10000.0
LAST = (((1,), (1,)), ((), ()))
FIRST = (((0,), (0,)), ((), ()))


def norm_rows(values):
    center = values - jnp.mean(values, axis=-1, keepdims=True)
    spread = jnp.mean(center * center, axis=-1, keepdims=True)
    factor = lax.rsqrt(spread + EPS)
    return (center * factor, factor)


def rotary_tables():
    half = ROT // 2
    rates = BASE ** (-2.0 * np.arange(half) / ROT)
    angles = np.arange(SEQ)[:, None] * rates[None, :]
    cosine = np.ones((SEQ, HD), np.float32)
    right = np.zeros((SEQ, HD), np.float32)
    left = np.zeros((SEQ, HD), np.float32)
    cosine[:, :half] = cosine[:, half:ROT] = np.cos(angles)
    right[:, :half] = -np.sin(angles)
    left[:, half:ROT] = np.sin(angles)
    return tuple(np.concatenate([one, one], axis=1) for one in (cosine, right, left))


def attend_kernel(scale, q_ref, k_ref, v_ref, qb_ref, kb_ref, vb_ref, ag_ref, cos_ref, sa_ref, sb_ref,
                  att_ref, jg_ref, bias_ref, q_s, k_s, v_s, dk_s, dv_s, dq_s):
    pair = pl.program_id(0)
    cols = jg_ref.shape[1] // 3
    half = ROT // 2
    lanes = 2 * HD
    block = QBLOCK
    low = lax.broadcasted_iota(jnp.int32, (SEQ, lanes), 1) < HD

    def rotary(x, sign):
        return (
            x * cos_ref[...]
            + sign * (pltpu.roll(x, lanes - half, 1) * sa_ref[...] + pltpu.roll(x, half, 1) * sb_ref[...])
        )

    q = (rotary(q_ref[...] + qb_ref[...], 1.0).astype(jnp.bfloat16) * scale).astype(jnp.bfloat16)
    k = rotary(k_ref[...] + kb_ref[...], 1.0).astype(jnp.bfloat16)
    v = (v_ref[...] + vb_ref[...]).astype(jnp.bfloat16)
    zero = jnp.zeros((SEQ, lanes), jnp.bfloat16)
    q_s[0] = jnp.where(low, q, zero)
    q_s[1] = jnp.where(low, zero, q)
    k_s[0] = jnp.where(low, k, zero)
    k_s[1] = jnp.where(low, zero, k)
    v_s[0] = jnp.where(low, v, zero)
    v_s[1] = jnp.where(low, zero, v)
    ag = ag_ref[...]
    nt = (((1,), (1,)), ((), ()))
    tn = (((0,), (0,)), ((), ()))
    keep = lax.broadcasted_iota(jnp.int32, (block, block), 0) <= lax.broadcasted_iota(
        jnp.int32, (block, block), 1
    )
    low_block = low[:block]
    for part in range(SEQ // block):
        begin, end = part * block, (part + 1) * block
        ag_rows = ag_ref[begin:end, :]
        att = jnp.zeros((block, lanes), jnp.float32)
        dq = jnp.zeros((block, lanes), jnp.float32)
        for head in range(2):
            q_rows = q_s[head, begin:end, :]
            ag_head = jnp.where(low_block if head == 0 else ~low_block, ag_rows, jnp.zeros_like(ag_rows))
            scores = lax.dot_general(k_s[head, :end, :], q_rows, nt, preferred_element_type=jnp.float32)
            diag = jnp.where(keep, scores[begin:end], MASKED)
            scores = diag if part == 0 else jnp.concatenate([scores[:begin], diag], axis=0)
            top = jnp.max(scores, axis=0, keepdims=True)
            expo = jnp.exp(scores - top)
            inverse = 1.0 / jnp.sum(expo, axis=0, keepdims=True)
            probs = expo * inverse
            probs16 = probs.astype(jnp.bfloat16)
            att += lax.dot_general(probs16, v_s[head, :end, :], tn, preferred_element_type=jnp.float32)
            dp = lax.dot_general(v_s[head, :end, :], ag_rows, nt, preferred_element_type=jnp.float32)
            delta = jnp.sum(probs * dp, axis=0, keepdims=True)
            ds = (probs * (dp - delta)).astype(jnp.bfloat16)
            dq += lax.dot_general(ds, k_s[head, :end, :], tn, preferred_element_type=jnp.float32)
            dk = lax.dot_general(ds, q_rows, (((1,), (0,)), ((), ())), preferred_element_type=jnp.float32)
            dv = lax.dot_general(probs16, ag_head, (((1,), (0,)), ((), ())), preferred_element_type=jnp.float32)
            first = head == 0
            if first:
                if begin:
                    dk_s[:begin, :] += dk[:begin]
                    dv_s[:begin, :] += dv[:begin]
                dk_s[begin:end, :] = dk[begin:]
                dv_s[begin:end, :] = dv[begin:]
            else:
                dk_s[:end, :] += dk
                dv_s[:end, :] += dv
        att_ref[begin:end, :] = att.astype(jnp.bfloat16)
        dq_s[begin:end, :] = dq * scale
    grads = (rotary(dq_s[...], -1.0), rotary(dk_s[...], -1.0), dv_s[...])
    for which in range(3):
        value = grads[which].astype(jnp.bfloat16)
        at = pl.ds(pl.multiple_of(which * cols + pair * lanes, lanes), lanes)
        jg_ref[:, at] = value
        bias_ref[which] = jnp.sum(value.astype(jnp.float32), axis=0, keepdims=True)


def attention(joined, bias, att_grad, scale):
    rows, cols = att_grad.shape
    lanes = 2 * HD
    pairs = cols // lanes
    seqs = rows // SEQ
    tables = rotary_tables()

    def part(which):
        return pl.BlockSpec((SEQ, lanes), lambda p: (0, which * pairs + p))

    def bias_part(which):
        return pl.BlockSpec((1, lanes), lambda p: (0, which * pairs + p))

    table = pl.BlockSpec((SEQ, lanes), lambda p: (0, 0))
    big = pltpu.VMEM((2, SEQ, lanes), jnp.bfloat16)
    run = pl.pallas_call(
        functools.partial(attend_kernel, scale),
        grid=(pairs,),
        in_specs=[part(0), part(1), part(2), bias_part(0), bias_part(1), bias_part(2), part(0), table, table, table],
        out_specs=[
            part(0),
            pl.BlockSpec((SEQ, 3 * cols), lambda p: (0, 0)),
            pl.BlockSpec((3, 1, lanes), lambda p: (0, 0, p)),
        ],
        out_shape=[
            jax.ShapeDtypeStruct((SEQ, cols), jnp.bfloat16),
            jax.ShapeDtypeStruct((SEQ, 3 * cols), jnp.bfloat16),
            jax.ShapeDtypeStruct((3, 1, cols), jnp.float32),
        ],
        scratch_shapes=[big, big, big] + [pltpu.VMEM((SEQ, lanes), jnp.float32)] * 3,
        compiler_params=pltpu.CompilerParams(vmem_limit_bytes=40 * 2**20),
        cost_estimate=pl.CostEstimate(
            flops=40 * SEQ * SEQ * cols, bytes_accessed=14 * SEQ * cols, transcendentals=SEQ * SEQ * cols // HD
        ),
        name="attention",
    )
    outs = []
    for s in range(seqs):
        at = slice(s * SEQ, (s + 1) * SEQ)
        j = joined[at]
        outs.append(run(j, j, j, bias, bias, bias, att_grad[at], *tables))
    if seqs == 1:
        return outs[0]
    return (
        jnp.concatenate([o[0] for o in outs]),
        jnp.concatenate([o[1] for o in outs]),
        sum(o[2] for o in outs),
    )


def local(
    tokens,
    cotangent,
    qkv_weight,
    qkv_bias,
    out_weight,
    out_bias,
    up_weight,
    up_bias,
    down_weight,
    down_bias,
    attn_gain,
    attn_shift,
    mlp_gain,
    mlp_shift,
):
    tp_count = lax.axis_size("tp")
    tp_index = lax.axis_index("tp")
    own_rows, width = tokens.shape
    cols = qkv_weight.shape[2]
    units = up_weight.shape[1]
    heads = cols // HD
    scale = HD ** (-0.5)
    all_tokens, grad_rows = (
        lax.all_gather(tokens, "tp", axis=0, tiled=True),
        lax.all_gather(cotangent, "tp", axis=0, tiled=True),
    )
    all_hat, all_factor = norm_rows(all_tokens.astype(jnp.float32))
    first_norm = (all_hat * attn_gain + attn_shift).astype(jnp.bfloat16)
    second_norm = (all_hat * mlp_gain + mlp_shift).astype(jnp.bfloat16)
    flat_qkv = qkv_weight.reshape(qkv_weight.shape[0], 3 * cols)

    flat_bias = qkv_bias.reshape(1, 3 * cols)
    qkv_all = lax.all_gather(flat_qkv, "fsdp", axis=0, tiled=True)
    out_all = lax.all_gather(out_weight, "fsdp", axis=0, tiled=True)
    up_all = lax.all_gather(up_weight, "fsdp", axis=0, tiled=True)
    down_all = lax.all_gather(down_weight, "fsdp", axis=0, tiled=True)
    att_grad16 = jnp.dot(grad_rows, out_all, preferred_element_type=jnp.float32).astype(jnp.bfloat16)
    joined = jnp.dot(first_norm, qkv_all, preferred_element_type=jnp.float32)
    attended, joined_grad, joined_sums = attention(joined, flat_bias, att_grad16, scale)
    up_pre = jnp.dot(second_norm, up_all, preferred_element_type=jnp.float32) + up_bias
    phi = 0.5 + 0.5 * lax.erf(up_pre * (0.5**0.5))
    activated = (up_pre * phi).astype(jnp.bfloat16)
    slope = phi + up_pre * jnp.exp(-0.5 * up_pre * up_pre) * ((0.5 / np.pi) ** 0.5)
    act_grad = jnp.dot(grad_rows, down_all, preferred_element_type=jnp.float32)
    pre_grad16 = (act_grad * slope).astype(jnp.bfloat16)
    block = lax.dot_general(attended, out_all, LAST, preferred_element_type=jnp.float32)
    block = block + lax.dot_general(activated, down_all, LAST, preferred_element_type=jnp.float32)
    branch = lax.psum_scatter(block, "tp", scatter_dimension=0, tiled=True)
    mixed = (tokens.astype(jnp.float32) + branch + (out_bias + down_bias)).astype(jnp.bfloat16)
    shard_rows = qkv_weight.shape[0]

    def cross(left, right):
        return lax.dot_general(left, right, FIRST, preferred_element_type=jnp.float32)

    def scattered(value):
        return lax.psum_scatter(
            value.astype(jnp.bfloat16), "fsdp", scatter_dimension=0, tiled=True
        ).astype(jnp.float32)

    up_weight_grad = scattered(cross(second_norm, pre_grad16))
    down_weight_grad = scattered(cross(grad_rows, activated))
    out_weight_grad = scattered(cross(grad_rows, attended))
    qkv_weight_grad = scattered(cross(first_norm, joined_grad)).reshape(shard_rows, 3, cols)
    first_block = lax.dot_general(joined_grad, qkv_all, LAST, preferred_element_type=jnp.float32)
    second_block = lax.dot_general(pre_grad16, up_all, LAST, preferred_element_type=jnp.float32)
    grad_own = cotangent.astype(jnp.float32)
    gain_terms = jnp.stack(
        [
            jnp.sum(first_block * all_hat, axis=0),
            jnp.sum(first_block, axis=0),
            jnp.sum(second_block * all_hat, axis=0),
            jnp.sum(second_block, axis=0),
            jnp.sum(grad_own, axis=0),
        ]
    )
    hat_grad = lax.psum_scatter(
        first_block * attn_gain + second_block * mlp_gain, "tp", scatter_dimension=0, tiled=True
    )
    hat_own = lax.dynamic_slice_in_dim(all_hat, tp_index * own_rows, own_rows, 0)
    factor_own = lax.dynamic_slice_in_dim(all_factor, tp_index * own_rows, own_rows, 0)
    center_grad = (
        hat_grad
        - jnp.mean(hat_grad, axis=-1, keepdims=True)
        - hat_own * jnp.mean(hat_grad * hat_own, axis=-1, keepdims=True)
    )
    tokens_grad = (grad_own + factor_own * center_grad).astype(jnp.bfloat16)
    qkv_bias_own = joined_sums.reshape(3, cols)
    up_bias_own = jnp.sum(pre_grad16, axis=0, dtype=jnp.float32)
    qkv_spread = lax.dynamic_update_slice_in_dim(
        jnp.zeros((3, width), jnp.float32), qkv_bias_own, tp_index * cols, 1
    )
    up_spread = lax.dynamic_update_slice_in_dim(
        jnp.zeros((units * tp_count,), jnp.float32), up_bias_own, tp_index * units, 0
    )
    gain_total, qkv_total, up_total = lax.psum((gain_terms, qkv_spread, up_spread), ("fsdp", "tp"))
    qkv_bias_grad = lax.dynamic_slice_in_dim(qkv_total, tp_index * cols, cols, 1)
    up_bias_grad = lax.dynamic_slice_in_dim(up_total, tp_index * units, units, 0)
    return (
        mixed,
        tokens_grad,
        qkv_weight_grad,
        qkv_bias_grad,
        out_weight_grad,
        gain_total[4],
        up_weight_grad,
        up_bias_grad,
        down_weight_grad,
        gain_total[4],
        gain_total[0],
        gain_total[1],
        gain_total[2],
        gain_total[3],
    )


def solution(mesh):
    return jax.shard_map(
        local,
        mesh=mesh,
        in_specs=(
            P(("fsdp", "tp"), None),
            P(("fsdp", "tp"), None),
            P("fsdp", None, "tp"),
            P(None, "tp"),
            P("fsdp", "tp"),
            P(),
            P("fsdp", "tp"),
            P("tp"),
            P("fsdp", "tp"),
            P(),
            P(),
            P(),
            P(),
            P(),
        ),
        out_specs=(
            P(("fsdp", "tp"), None),
            P(("fsdp", "tp"), None),
            P("fsdp", None, "tp"),
            P(None, "tp"),
            P("fsdp", "tp"),
            P(),
            P("fsdp", "tp"),
            P("tp"),
            P("fsdp", "tp"),
            P(),
            P(),
            P(),
            P(),
            P(),
        ),
        check_vma=False,
    )
```

time: 595 us -> 680 us (1.14)
  waiting for transfers between devices: 272 us -> 463 us
  matrix products: 155 us -> 79 us
  other arithmetic: 61.1 us -> 15.9 us
  Pallas kernels: 0 us -> 35.6 us
  local copies, waits for them, and re-layouts: 44.1 us -> 25.3 us
    unnamed x9 -> x14, waiting for transfers between devices: 3.18 us -> 91.6 us
    dot_general x20 -> x8, matrix products: 134 us -> 56.7 us  [the longest x1 10.6 us: local(): act_grad = jnp.dot(grad_rows, down_all, preferred_element_type=jnp.float32)]
    reduce_scatter x1, waiting for transfers between devices: 0.02 us -> 53.9 us  [local(): lax.psum_scatter(first_block * attn_gain + second_block * mlp_gain, 'tp',...]
    pallas_call x0 -> x1, Pallas kernels: none -> 35.6 us  [attention(): outs.append(run(j, j, j, bias, bias, bias, att_grad[at], *tables))]
    slice x14 -> x0, local copies, waits for them, and re-layouts: 24.2 us -> none  [the longest x2 5.43 us: local(): joined[:, cols:2 * cols].reshape(rows_all, heads, HD)]
    reduce_scatter x2 -> x3, waiting for transfers between devices: 126 us -> 150 us  [the longest x2 141 us: scattered(): lax.psum_scatter(value.astype(jnp.bfloat16), 'fsdp', scatter_dimension=0,...]
    convert_element_type x4 -> x1, other arithmetic: 25.5 us -> 1.78 us  [scattered(): return lax.psum_scatter(value.astype(jnp.bfloat16), 'fsdp', scatter_dimen...]
    all_gather x4, waiting for transfers between devices: 79.8 us -> 102 us  [the longest x1 43.9 us: local(): qkv_all = lax.all_gather(flat_qkv, 'fsdp', axis=0, tiled=True)]
  transfers between devices with their start and end apart: 9 -> 12, of which waited for: 5 -> 11; matrix products, arithmetic and copies ran while one was open for 35% -> 16% of each run, Pallas kernels for 0% -> 5%
where the time goes in v1:
time: 680 us; the launch traced here: 675 us
  waiting for transfers between devices  463 us (68%)
  matrix products  79 us (12%)
  blocking collectives  40.6 us (6%)
  Pallas kernels  35.6 us (5%)
  local copies, waits for them, and re-layouts  25.3 us (4%)
  other arithmetic  15.9 us (2%)
  between operations  15 us (2%)
    reduce_scatter x2, waiting for transfers between devices, scattered(): lax.psum_scatter(value.astype(jnp.bfloat16), 'fsdp', scatter_dimension=0,...  141 us
    unnamed x14, waiting for transfers between devices  91.6 us
    reduce_scatter x1, waiting for transfers between devices, local(): lax.psum_scatter(first_block * attn_gain + second_block * mlp_gain, 'tp',...  53.9 us
    all_gather x1, waiting for transfers between devices, local(): qkv_all = lax.all_gather(flat_qkv, 'fsdp', axis=0, tiled=True)  43.9 us
    psum x1, blocking collectives, local(): lax.psum((gain_terms, qkv_spread, up_spread), ('fsdp', 'tp'))  40.6 us
    all_gather x1, waiting for transfers between devices, local(): out_all = lax.all_gather(out_weight, 'fsdp', axis=0, tiled=True)  35.9 us
    pallas_call x1, Pallas kernels, attention(): outs.append(run(j, j, j, bias, bias, bias, att_grad[at], *tables))  35.6 us
    all_gather x1, waiting for transfers between devices, local(): lax.all_gather(cotangent, 'tp', axis=0, tiled=True)  33.6 us
  transfers between devices with their start and end apart: 12, of which 11 were waited for; matrix products, arithmetic and copies ran while one was open for 16% of the time, Pallas kernels for 5%

profile of v1, /device:TPU:0, one launch (start us, length us, event | category | flops | bytes accessed | tf_op | source)
XLA Modules:
  0.0 675.0 jit_solution(13878892715723949030)
XLA Ops:
  7.2 0.7 all-gather.7.cloned.1.call-update
  8.0 0.7 all-gather.13.cloned.1.call-update
  8.7 0.7 all-gather.11.cloned.1.call-update
  9.4 0.0 all-gather.9.cloned.1.call-start
  9.4 1.6 copy.48
  11.1 0.0 all-gather.15.cloned.1.call-start
  11.1 0.5 all-gather.15.cloned.1.call-update
  11.7 0.5 all-gather.17.cloned.1.call-update
  12.3 0.7 copy.49
  13.0 32.4 %all-gather.7.cloned.1.call-done = bf16[1024,1024]{1,0:T(8,128)(2,1)} async-done(((bf16[512,1024]{1,0:T(8,128)(2,1)}), bf16[1024,1024]{1,0:T(8,128)(2,1)}) %all-gather.7.cloned.1.call-update) | async-done | bytes 2097168 | tf_op jit(solution)/shard_map/all_gather | solution.py:193
  45.4 1.9 convert_reduce_fusion.1
  47.3 2.3 fusion.8
  49.7 35.9 %all-gather.13.cloned.1.call-done = bf16[1024,512]{1,0:T(8,128)(2,1)} async-done(((bf16[64,512]{1,0:T(8,128)(2,1)}), bf16[1024,512]{1,0:T(8,128)(2,1)}) %all-gather.13.cloned.1.call-update) | async-done | bytes 1048592 | tf_op jit(solution)/shard_map/all_gather | solution.py:203
  85.5 33.6 %all-gather.11.cloned.1.call-done = bf16[1024,1024]{1,0:T(8,128)(2,1)} async-done(((bf16[512,1024]{1,0:T(8,128)(2,1)}), bf16[1024,1024]{1,0:T(8,128)(2,1)}) %all-gather.11.cloned.1.call-update) | async-done | bytes 2097168 | tf_op jit(solution)/shard_map/all_gather | solution.py:194
  119.2 4.1 convolution_convert_fusion.3.ag_ref
  123.2 43.9 %all-gather.9.cloned.1.call-done = bf16[1024,1536]{1,0:T(8,128)(2,1)} async-done(((bf16[64,1536]{1,0:T(8,128)(2,1)}), bf16[1024,1536]{1,0:T(8,128)(2,1)}) %all-gather.9.cloned.1.call-update) | async-done | bytes 3145744 | tf_op jit(solution)/shard_map/all_gather | solution.py:202
  167.1 6.2 fusion.11.q_ref.k_ref.v_ref
  173.3 35.6 %attention.1 = (bf16[1024,512]{1,0:T(8,128)(2,1)S(1)}, bf16[1024,1536]{1,0:T(8,128)(2,1)S(1)}, f32[3,1,512]{2,1,0:T(1,128)S(1)}) custom-call(f32[1024,1536]{1,0:T(8,128)S(1)} %fusion.11.q_ref.k_ref.v_ref, f32[1024,1536]{1,0:T(8,128)S(1)} %fusion.11.q_ref.k_ref.v_ref, f32[1024,1536]{1,0:T(8,128)S(1)} %fusion.11.q_ref.k_ref.v_ref, f32[1,1536]{1,0:T(1,128)S(1)} %bitcast.47, ...), custom_call_target="tpu_custom_call" | custom-call | flops 21474836480 | bytes 7340032 | tf_op jit(solution)/shard_map/attention/pallas_call | solution.py:159
  209.0 1.7 copy-done.4
  210.7 2.2 fusion.10
  212.9 2.3 copy.42
  215.2 0.0 reduce-scatter.15.cloned.1.call-start
  215.3 7.1 %convolution_convert_fusion = bf16[1024,1536]{1,0:T(8,128)(2,1)} fusion(bf16[1024,1536]{1,0:T(8,128)(2,1)} %copy-done.4, bf16[1024,1024]{1,0:T(8,128)(2,1)S(1)} %copy-done.6, f32[1024]{0:T(1024)S(1)} %copy-done.17, f32[1024]{0:T(1024)S(1)} %copy-done.19, f32[1024]{0:T(1024)S(1)} %add_rsqrt_fusion, f32[1024]{0:T(1024)S(1)} %broadcast_multiply_fusion), kind=kOutput, calls=%fused_computation.21 | convolution fusion | flops 3229089792 | bytes 8404992 | tf_op jit(solution)/shard_map/dot_general | solution.py:222
  222.4 0.0 reduce-scatter.21.cloned.1.call-start
  222.5 10.4 %multiply_convert_fusion = (bf16[1024,2048]{1,0:T(8,128)(2,1)S(1)}, f32[1024,2048]{1,0:T(8,128)}) fusion(f32[2048]{0:T(1024)S(1)} %copy-done.16, bf16[1024,2048]{1,0:T(8,128)(2,1)} %all-gather.15.cloned.1.call-done, bf16[1024,1024]{1,0:T(8,128)(2,1)S(1)} %copy-done.6, f32[1024]{0:T(1024)S(1)} %copy-done.18, f32[1024]{0:T(1024)S(1)} %copy-done.20, ...), kind=kOutput, calls=%fused_computation.8 | convolution fusion | flops 4313841664 | bytes 18898944 | tf_op jit(solution)/shard_map/dot_general | solution.py:209
  232.9 2.0 copy-done.23
  234.9 6.2 convert_bitcast_fusion
  241.1 6.7 copy.44
  247.9 0.0 reduce-scatter.17.cloned.1.call-start
  247.9 21.9 %all-gather.17.cloned.1.call-done = bf16[1024,2048]{1,0:T(8,128)(2,1)} async-done(((bf16[64,2048]{1,0:T(8,128)(2,1)}), bf16[1024,2048]{1,0:T(8,128)(2,1)}) %all-gather.17.cloned.1.call-update) | async-done | bytes 4194320 | tf_op jit(solution)/shard_map/all_gather | solution.py:205
  269.8 10.6 %convert_reduce_fusion = (f32[2048]{0:T(1024)S(1)}, bf16[1024,2048]{1,0:T(8,128)(2,1)S(1)}) fusion(f32[1024,2048]{1,0:T(8,128)} %get-tuple-element.83, f32[2048]{0:T(1024)S(1)} %copy-done.16, bf16[1024,1024]{1,0:T(8,128)(2,1)} %all-gather.11.cloned.1.call-done, bf16[1024,2048]{1,0:T(8,128)(2,1)} %all-gather.17.cloned.1.call-done), kind=kOutput, calls=%fused_computation.7 | convolution fusion | flops 4322228224 | bytes 18890752 | tf_op jit(solution)/shard_map/dot_general | solution.py:213
  280.4 2.0 copy-done.21
  282.4 6.8 %convolution_convert_fusion.1 = bf16[1024,2048]{1,0:T(8,128)(2,1)} fusion(bf16[1024,2048]{1,0:T(8,128)(2,1)S(1)} %get-tuple-element.85, bf16[1024,1024]{1,0:T(8,128)(2,1)S(1)} %copy-done.6, f32[1024]{0:T(1024)S(1)} %copy-done.18, f32[1024]{0:T(1024)S(1)} %copy-done.20, f32[1024]{0:T(1024)S(1)} %add_rsqrt_fusion, f32[1024]{0:T(1024)S(1)} %broadcast_multiply_fusion), kind=kOutput, calls=%fused_computation.22 | convolution fusion | flops 4303355904 | bytes 10502144 | tf_op jit(solution)/shard_map/dot_general | solution.py:222
  289.2 0.3 reduce-scatter.13.cloned.1.call-start
  289.5 6.5 fusion.18
  296.0 7.9 %fusion.13 = (f32[1024]{0:T(1024)S(1)}, f32[1024]{0:T(1024)S(1)}, f32[1024,1024]{1,0:T(8,128)}, f32[1024]{0:T(1024)S(1)}, f32[1024]{0:T(1024)S(1)}, /*index=5*/f32[1024,1024]{1,0:T(8,128)}) fusion(f32[1024]{0:T(1024)S(1)} %add_rsqrt_fusion, f32[1024]{0:T(1024)S(1)} %broadcast_multiply_fusion, bf16[1024,1024]{1,0:T(8,128)(2,1)S(1)} %copy-done.6, ...), kind=kOutput, calls=%fused_computation.41 | convolution fusion | flops 4307546112 | bytes 23101440 | tf_op jit(solution)/shard_map/dot_general | solution.py:234
  303.9 0.0 reduce-scatter.11.cloned.1.call-start
  304.0 7.7 %fusion.17 = f32[1024,1024]{1,0:T(8,128)S(1)} fusion(bf16[1024,2048]{1,0:T(8,128)(2,1)} %copy-done.23, bf16[1024,2048]{1,0:T(8,128)(2,1)} %all-gather.17.cloned.1.call-done), kind=kOutput, calls=%fused_computation.45 | convolution fusion | flops 4294967296 | bytes 12582912 | tf_op jit(solution)/shard_map/dot_general | solution.py:216
  311.7 3.3 convolution_add_fusion
  315.1 0.7 copy-done.13
  315.7 0.1 dynamic-slice.3
  315.8 14.1 %reduce-scatter.19.cloned.1.call-done = bf16[64,512]{1,0:T(8,128)(2,1)} async-done(((bf16[1024,512]{1,0:T(8,128)(2,1)}), bf16[64,512]{1,0:T(8,128)(2,1)}) %reduce-scatter.19.cloned.1.call-update) | async-done | bytes 65552
  329.9 1.0 copy.43
  330.9 0.8 copy.40
  331.6 0.2 dynamic_update_slice.7
  331.8 67.6 %reduce-scatter.15.cloned.1.call-done = bf16[64,1536]{1,0:T(8,128)(2,1)} async-done(((bf16[1024,1536]{1,0:T(8,128)(2,1)}), bf16[64,1536]{1,0:T(8,128)(2,1)}) %reduce-scatter.15.cloned.1.call-update) | async-done | bytes 196624 | tf_op jit(solution)/shard_map/reduce_scatter | solution.py:225
  399.5 1.0 reshape.89
  400.4 0.8 copy.52
  401.2 74.3 %reduce-scatter.21.cloned.1.call-done = bf16[64,2048]{1,0:T(8,128)(2,1)} async-done(((bf16[1024,2048]{1,0:T(8,128)(2,1)}), bf16[64,2048]{1,0:T(8,128)(2,1)}) %reduce-scatter.21.cloned.1.call-update) | async-done | bytes 262160
  475.5 1.2 copy.45
  476.7 1.0 copy.41
  477.7 72.9 %reduce-scatter.17.cloned.1.call-done = bf16[64,2048]{1,0:T(8,128)(2,1)} async-done(((bf16[1024,2048]{1,0:T(8,128)(2,1)}), bf16[64,2048]{1,0:T(8,128)(2,1)}) %reduce-scatter.17.cloned.1.call-update) | async-done | bytes 262160 | tf_op jit(solution)/shard_map/reduce_scatter | solution.py:225
  550.6 1.8 convert_element_type.76
  552.4 53.9 %reduce-scatter.13.cloned.1.call-done = f32[512,1024]{1,0:T(8,128)} async-done(((f32[1024,1024]{1,0:T(8,128)}), f32[512,1024]{1,0:T(8,128)}) %reduce-scatter.13.cloned.1.call-update) | async-done | bytes 2097168 | tf_op jit(solution)/shard_map/reduce_scatter | solution.py:245
  606.3 2.7 fusion.15
  609.1 0.1 copy-done.5
  609.2 3.3 convert_reduce_fusion.2
  612.5 40.6 %all-reduce = (f32[3,1024]{1,0:T(4,128)S(1)}, f32[5,1024]{1,0:T(8,128)S(1)}, f32[4096]{0:T(1024)S(1)}) all-reduce(f32[3,1024]{1,0:T(4,128)S(1)} %bitcast_dynamic-update-slice_fusion, f32[5,1024]{1,0:T(8,128)S(1)} %stack.23, f32[4096]{0:T(1024)S(1)} %dynamic_update_slice.7), channel_id=1, replica_groups=mesh['fsdp'=16,'tp'=2] {'fsdp','tp'}, use_global_device_ids=true, to_apply=%region_7.0 | all-reduce | flops 12288 | bytes 98304 | tf_op jit(solution)/shard_map/psum | solution.py:264
  653.1 0.6 dynamic_slice.12
  653.7 0.6 fusion.16
  654.3 0.6 constant_dynamic-slice_fusion
  654.9 9.3 %reduce-scatter.11.cloned.1.call-done = f32[512,1024]{1,0:T(8,128)} async-done(((f32[1024,1024]{1,0:T(8,128)}), f32[512,1024]{1,0:T(8,128)}) %reduce-scatter.11.cloned.1.call-update) | async-done | bytes 2097168 | tf_op jit(solution)/shard_map/reduce_scatter | solution.py:217
  664.2 2.9 add_convert_fusion.2
  667.2 0.6 copy.56
  (64 shorter events, 0.5 us)
Async XLA Ops:
  7.2 38.2 %all-gather.7.cloned.1.call-start = ((), (), s32[]{:S(2)}) async-start(), calls=%async_computation.6 | async-start | bytes 3145728 | tf_op jit(solution)/shard_map/all_gather | solution.py:193
  7.9 77.6 %all-gather.13.cloned.1.call-start = ((), (), s32[]{:S(2)}) async-start(), calls=%async_computation.9 | async-start | bytes 1114112 | tf_op jit(solution)/shard_map/all_gather | solution.py:203
  8.7 110.5 %all-gather.11.cloned.1.call-start = ((), (), s32[]{:S(2)}) async-start(), calls=%async_computation.8 | async-start | bytes 3145728 | tf_op jit(solution)/shard_map/all_gather | solution.py:194
  9.4 157.7 %all-gather.9.cloned.1.call-start = ((), (), s32[]{:S(2)}) async-start(), calls=%async_computation.7 | async-start | bytes 3342336 | tf_op jit(solution)/shard_map/all_gather | solution.py:202
  11.1 211.4 %all-gather.15.cloned.1.call-start = ((), (), s32[]{:S(2)}) async-start(), calls=%async_computation.10 | async-start | bytes 4456448 | tf_op jit(solution)/shard_map/all_gather | solution.py:204
  11.7 258.1 %all-gather.17.cloned.1.call-start = ((), (), s32[]{:S(2)}) async-start(), calls=%async_computation.11 | async-start | bytes 4456448 | tf_op jit(solution)/shard_map/all_gather | solution.py:205
  12.3 317.6 %reduce-scatter.19.cloned.1.call-start = ((), (), s32[]{:S(2)}) async-start(), calls=%async_computation.16 | async-start | bytes 1114112
  49.6 117.5 %copy-start.17 = (f32[1024]{0:T(1024)S(1)}, f32[1024]{0:T(1024)}, u32[]{:S(2)}) copy-start(f32[1024]{0:T(1024)} %param.28) | copy-start | bytes 12292
  49.7 117.5 %copy-start.19 = (f32[1024]{0:T(1024)S(1)}, f32[1024]{0:T(1024)}, u32[]{:S(2)}) copy-start(f32[1024]{0:T(1024)} %param.27) | copy-start | bytes 12292
  123.2 50.1 %copy-start = (f32[1024,128]{1,0:T(8,128)S(1)}, f32[1024,128]{1,0:T(8,128)}, u32[]{:S(2)}) copy-start(f32[1024,128]{1,0:T(8,128)} %constant.43.clone.sb_ref) | copy-start | bytes 1572868
  123.2 50.1 %copy-start.1 = (f32[1024,128]{1,0:T(8,128)S(1)}, f32[1024,128]{1,0:T(8,128)}, u32[]{:S(2)}) copy-start(f32[1024,128]{1,0:T(8,128)} %constant.42.clone.sa_ref) | copy-start | bytes 1572868
  123.2 50.1 %copy-start.2 = (f32[1024,128]{1,0:T(8,128)S(1)}, f32[1024,128]{1,0:T(8,128)}, u32[]{:S(2)}) copy-start(f32[1024,128]{1,0:T(8,128)} %constant.41.clone.cos_ref) | copy-start | bytes 1572868
  167.1 6.2 copy-start.3
  173.3 37.4 %copy-start.9 = (bf16[1024,1024]{1,0:T(8,128)(2,1)S(1)}, bf16[1024,1024]{1,0:T(8,128)(2,1)}, u32[]{:S(2)}) copy-start(bf16[1024,1024]{1,0:T(8,128)(2,1)} %all-gather.11.cloned.1.call-done) | copy-start | bytes 6291460
  209.0 1.7 copy-start.4
  210.7 4.6 copy-start.6
  215.2 184.2 %reduce-scatter.15.cloned.1.call-start = ((), (), s32[]{:S(2)}) async-start(), calls=%async_computation.14 | async-start | bytes 3342336 | tf_op jit(solution)/shard_map/reduce_scatter | solution.py:225
  215.3 7.2 %copy-start.16 = (f32[2048]{0:T(1024)S(1)}, f32[2048]{0:T(1024)}, u32[]{:S(2)}) copy-start(f32[2048]{0:T(1024)} %param.24) | copy-start | bytes 24580
  215.3 7.2 %copy-start.18 = (f32[1024]{0:T(1024)S(1)}, f32[1024]{0:T(1024)}, u32[]{:S(2)}) copy-start(f32[1024]{0:T(1024)} %param.30) | copy-start | bytes 12292
  215.3 7.2 %copy-start.20 = (f32[1024]{0:T(1024)S(1)}, f32[1024]{0:T(1024)}, u32[]{:S(2)}) copy-start(f32[1024]{0:T(1024)} %param.29) | copy-start | bytes 12292
  222.4 253.1 %reduce-scatter.21.cloned.1.call-start = ((), (), s32[]{:S(2)}) async-start(), calls=%async_computation.17 | async-start | bytes 4456448
  222.5 12.4 %copy-start.10 = (bf16[1024,1024]{1,0:T(8,128)(2,1)S(1)}, bf16[1024,1024]{1,0:T(8,128)(2,1)}, u32[]{:S(2)}) copy-start(bf16[1024,1024]{1,0:T(8,128)(2,1)} %all-gather.11.cloned.1.call-done) | copy-start | bytes 6291460
  232.9 2.0 copy-start.23
  247.9 302.7 %reduce-scatter.17.cloned.1.call-start = ((), (), s32[]{:S(2)}) async-start(), calls=%async_computation.15 | async-start | bytes 4456448 | tf_op jit(solution)/shard_map/reduce_scatter | solution.py:225
  280.4 2.0 copy-start.21
  289.2 317.1 %reduce-scatter.13.cloned.1.call-start = ((), (), s32[]{:S(2)}) async-start(), calls=%async_computation.13 | async-start | bytes 6291456 | tf_op jit(solution)/shard_map/reduce_scatter | solution.py:245
  289.5 6.5 copy-start.15
  289.5 6.5 copy-start.22
  303.9 7.8 %copy-start.11 = (bf16[1024,512]{1,0:T(8,128)(2,1)S(1)}, bf16[1024,512]{1,0:T(8,128)(2,1)}, u32[]{:S(2)}) copy-start(bf16[1024,512]{1,0:T(8,128)(2,1)} %all-gather.13.cloned.1.call-done) | copy-start | bytes 3145732
  303.9 360.3 %reduce-scatter.11.cloned.1.call-start = ((), (), s32[]{:S(2)}) async-start(), calls=%async_computation.12 | async-start | bytes 6291456 | tf_op jit(solution)/shard_map/reduce_scatter | solution.py:217
  315.0 0.7 copy-start.13
  315.0 0.7 copy-start.14
  330.9 278.2 %copy-start.8 = (bf16[512,1024]{1,0:T(8,128)(2,1)S(1)}, bf16[512,1024]{1,0:T(8,128)(2,1)}, u32[]{:S(2)}) copy-start(bf16[512,1024]{1,0:T(8,128)(2,1)} %param.18) | copy-start | bytes 3145732
  606.3 2.9 copy-start.5
  609.1 55.2 %copy-start.7 = (bf16[512,1024]{1,0:T(8,128)(2,1)S(1)}, bf16[512,1024]{1,0:T(8,128)(2,1)}, u32[]{:S(2)}) copy-start(bf16[512,1024]{1,0:T(8,128)(2,1)} %param.17) | copy-start | bytes 3145732
  654.3 13.5 %copy-start.12 = (f32[1,1024]{1,0:T(1,128)}, f32[1,1024]{1,0:T(1,128)S(1)}, u32[]{:S(2)}) copy-start(f32[1,1024]{1,0:T(1,128)S(1)} %get-tuple-element.81) | copy-start | bytes 12292
Sparse Core Ops, SparseCore 0:
  9.6 35.7 all-gather.6
  47.6 37.9 all-gather.12
  87.1 32.0 all-gather.10
  121.9 45.1 all-gather.8
  169.1 49.5 all-gather.14
  220.7 49.0 all-gather.16
  274.0 55.8 reduce-scatter.18
  334.2 65.2 reduce-scatter.14
  403.8 71.5 reduce-scatter.20
  479.2 71.3 reduce-scatter.16
  553.0 53.2 reduce-scatter.12
  608.4 55.7 reduce-scatter.10

commit v2 on v1

--- a/solution.py
+++ b/solution.py
@@ -166,6 +166,78 @@
     )
 
 
+def bits_of(name):
+    return (lax.axis_size(name) - 1).bit_length()
+
+
+def swap(value, name, bit):
+    size = lax.axis_size(name)
+    return lax.ppermute(value, name, [(i, i ^ (1 << bit)) for i in range(size)])
+
+
+def own_bit(name, bit):
+    return (lax.axis_index(name) >> bit) & 1
+
+
+def gather_rows(value, name):
+    rows, width = value.shape
+    count = bits_of(name)
+    for step in range(count):
+        bit = count - 1 - step
+        other = swap(value, name, bit)
+        upper = own_bit(name, bit) == 1
+        value = jnp.stack([jnp.where(upper, other, value), jnp.where(upper, value, other)], axis=step)
+    return value.reshape(rows << count, width)
+
+
+def after(value, *earlier):
+    return lax.optimization_barrier((value,) + earlier)[0]
+
+
+def halve_send(value, name, bit):
+    axis = bits_of(name) - 1 - bit
+    mine = own_bit(name, bit)
+    kept = lax.dynamic_index_in_dim(value, mine, axis, keepdims=False)
+    sent = lax.dynamic_index_in_dim(value, 1 - mine, axis, keepdims=False)
+    return kept, swap(sent.astype(jnp.bfloat16), name, bit)
+
+
+class Scatter:
+    def __init__(self, value, name, carry):
+        self.name, self.carry, self.bit = name, carry, 0
+        self.count = bits_of(name)
+        rows, width = value.shape
+        self.value = value.reshape((2,) * self.count + (rows >> self.count, width))
+        self.send()
+
+    def send(self):
+        self.kept, self.got = halve_send(self.value, self.name, self.bit)
+        self.bit += 1
+
+    def step(self, *earlier):
+        if self.bit > self.count:
+            return
+        got = after(self.got, *earlier) if earlier else self.got
+        value = self.kept.astype(jnp.float32) + got.astype(jnp.float32)
+        if self.bit < self.count:
+            self.value = value.astype(self.carry)
+            self.send()
+        else:
+            self.value = value
+            self.bit += 1
+
+    def result(self, *earlier):
+        while self.bit <= self.count:
+            self.step(*earlier)
+        return self.value
+
+
+def sum_over(value, name):
+    for bit in range(bits_of(name)):
+        value = value + swap(value, name, bit)
+    return value
+
+
 def local(
     tokens,
     cotangent,
@@ -182,7 +254,6 @@
     mlp_gain,
     mlp_shift,
 ):
-    tp_count = lax.axis_size("tp")
     tp_index = lax.axis_index("tp")
     own_rows, width = tokens.shape
     cols = qkv_weight.shape[2]
@@ -190,8 +261,8 @@
     heads = cols // HD
     scale = HD ** (-0.5)
     all_tokens, grad_rows = (
-        lax.all_gather(tokens, "tp", axis=0, tiled=True),
-        lax.all_gather(cotangent, "tp", axis=0, tiled=True),
+        gather_rows(tokens, "tp"),
+        gather_rows(cotangent, "tp"),
     )
     all_hat, all_factor = norm_rows(all_tokens.astype(jnp.float32))
     first_norm = (all_hat * attn_gain + attn_shift).astype(jnp.bfloat16)
@@ -199,39 +270,57 @@
     flat_qkv = qkv_weight.reshape(qkv_weight.shape[0], 3 * cols)
 
     flat_bias = qkv_bias.reshape(1, 3 * cols)
-    qkv_all = lax.all_gather(flat_qkv, "fsdp", axis=0, tiled=True)
-    out_all = lax.all_gather(out_weight, "fsdp", axis=0, tiled=True)
-    up_all = lax.all_gather(up_weight, "fsdp", axis=0, tiled=True)
-    down_all = lax.all_gather(down_weight, "fsdp", axis=0, tiled=True)
+    first_all = lax.all_gather(
+        jnp.concatenate([flat_qkv, out_weight], axis=1), "fsdp", axis=0, tiled=True
+    )
+    second_all = lax.all_gather(
+        jnp.concatenate([up_weight, down_weight], axis=1), "fsdp", axis=0, tiled=True
+    )
+    qkv_all, out_all = first_all[:, : 3 * cols], first_all[:, 3 * cols :]
+    up_all, down_all = second_all[:, :units], second_all[:, units:]
+
+    def cross(left, right):
+        return lax.dot_general(left, right, FIRST, preferred_element_type=jnp.float32).astype(
+            jnp.bfloat16
+        )
+
     att_grad16 = jnp.dot(grad_rows, out_all, preferred_element_type=jnp.float32).astype(jnp.bfloat16)
     joined = jnp.dot(first_norm, qkv_all, preferred_element_type=jnp.float32)
     attended, joined_grad, joined_sums = attention(joined, flat_bias, att_grad16, scale)
+    first = Scatter(
+        jnp.concatenate([cross(first_norm, joined_grad), cross(grad_rows, attended)], axis=1),
+        "fsdp",
+        jnp.bfloat16,
+    )
+    first_block = lax.dot_general(joined_grad, qkv_all, LAST, preferred_element_type=jnp.float32)
+    first.step(first_block)
     up_pre = jnp.dot(second_norm, up_all, preferred_element_type=jnp.float32) + up_bias
     phi = 0.5 + 0.5 * lax.erf(up_pre * (0.5**0.5))
     activated = (up_pre * phi).astype(jnp.bfloat16)
     slope = phi + up_pre * jnp.exp(-0.5 * up_pre * up_pre) * ((0.5 / np.pi) ** 0.5)
-    act_grad = jnp.dot(grad_rows, down_all, preferred_element_type=jnp.float32)
+    down_cross = cross(grad_rows, activated)
+    down_weight_grad = lax.psum_scatter(down_cross, "fsdp", scatter_dimension=0, tiled=True).astype(
+        jnp.float32
+    )
+    first.step(down_cross)
+    act_grad = jnp.dot(after(grad_rows, down_cross), down_all, preferred_element_type=jnp.float32)
     pre_grad16 = (act_grad * slope).astype(jnp.bfloat16)
-    block = lax.dot_general(attended, out_all, LAST, preferred_element_type=jnp.float32)
+    up_cross = cross(second_norm, pre_grad16)
+    up = Scatter(up_cross, "fsdp", jnp.bfloat16)
+    first.step(up_cross)
+    up_bias_own = jnp.sum(pre_grad16, axis=0, dtype=jnp.float32)
+    second_block = lax.dot_general(
+        after(pre_grad16, up.got), up_all, LAST, preferred_element_type=jnp.float32
+    )
+    up.step()
+    hat_terms = Scatter(first_block * attn_gain + second_block * mlp_gain, "tp", jnp.float32)
+    first.step(second_block)
+    block = lax.dot_general(
+        after(attended, second_block), out_all, LAST, preferred_element_type=jnp.float32
+    )
     block = block + lax.dot_general(activated, down_all, LAST, preferred_element_type=jnp.float32)
-    branch = lax.psum_scatter(block, "tp", scatter_dimension=0, tiled=True)
-    mixed = (tokens.astype(jnp.float32) + branch + (out_bias + down_bias)).astype(jnp.bfloat16)
-    shard_rows = qkv_weight.shape[0]
-
-    def cross(left, right):
-        return lax.dot_general(left, right, FIRST, preferred_element_type=jnp.float32)
-
-    def scattered(value):
-        return lax.psum_scatter(
-            value.astype(jnp.bfloat16), "fsdp", scatter_dimension=0, tiled=True
-        ).astype(jnp.float32)
-
-    up_weight_grad = scattered(cross(second_norm, pre_grad16))
-    down_weight_grad = scattered(cross(grad_rows, activated))
-    out_weight_grad = scattered(cross(grad_rows, attended))
-    qkv_weight_grad = scattered(cross(first_norm, joined_grad)).reshape(shard_rows, 3, cols)
-    first_block = lax.dot_general(joined_grad, qkv_all, LAST, preferred_element_type=jnp.float32)
-    second_block = lax.dot_general(pre_grad16, up_all, LAST, preferred_element_type=jnp.float32)
+    branch_terms = Scatter(block, "tp", jnp.float32)
+    up.step(block)
     grad_own = cotangent.astype(jnp.float32)
     gain_terms = jnp.stack(
         [
@@ -242,9 +331,13 @@
             jnp.sum(grad_own, axis=0),
         ]
     )
-    hat_grad = lax.psum_scatter(
-        first_block * attn_gain + second_block * mlp_gain, "tp", scatter_dimension=0, tiled=True
-    )
+    small = sum_over(
+        jnp.concatenate([gain_terms.reshape(-1), joined_sums.reshape(-1), up_bias_own]), "fsdp"
+    )
+    gain_total = sum_over(small[: 5 * width], "tp").reshape(5, width)
+    qkv_bias_grad = small[5 * width : 5 * width + 3 * cols].reshape(3, cols)
+    up_bias_grad = small[5 * width + 3 * cols :]
+    hat_grad = hat_terms.result(gain_terms)
     hat_own = lax.dynamic_slice_in_dim(all_hat, tp_index * own_rows, own_rows, 0)
     factor_own = lax.dynamic_slice_in_dim(all_factor, tp_index * own_rows, own_rows, 0)
     center_grad = (
@@ -253,17 +346,13 @@
         - hat_own * jnp.mean(hat_grad * hat_own, axis=-1, keepdims=True)
     )
     tokens_grad = (grad_own + factor_own * center_grad).astype(jnp.bfloat16)
-    qkv_bias_own = joined_sums.reshape(3, cols)
-    up_bias_own = jnp.sum(pre_grad16, axis=0, dtype=jnp.float32)
-    qkv_spread = lax.dynamic_update_slice_in_dim(
-        jnp.zeros((3, width), jnp.float32), qkv_bias_own, tp_index * cols, 1
-    )
-    up_spread = lax.dynamic_update_slice_in_dim(
-        jnp.zeros((units * tp_count,), jnp.float32), up_bias_own, tp_index * units, 0
-    )
-    gain_total, qkv_total, up_total = lax.psum((gain_terms, qkv_spread, up_spread), ("fsdp", "tp"))
-    qkv_bias_grad = lax.dynamic_slice_in_dim(qkv_total, tp_index * cols, cols, 1)
-    up_bias_grad = lax.dynamic_slice_in_dim(up_total, tp_index * units, units, 0)
+    branch = branch_terms.result(gain_terms)
+    mixed = (tokens.astype(jnp.float32) + branch + (out_bias + down_bias)).astype(jnp.bfloat16)
+    shard_rows = qkv_weight.shape[0]
+    first_sums = first.result(gain_terms)
+    up_weight_grad = up.result(gain_terms)
+    qkv_weight_grad = first_sums[:, : 3 * cols].reshape(shard_rows, 3, cols)
+    out_weight_grad = first_sums[:, 3 * cols :]
     return (
         mixed,
         tokens_grad,

time: 680 us -> 319 us (0.47)
  waiting for transfers between devices: 463 us -> 114 us
  blocking collectives: 40.6 us -> 0 us
  starting transfers between devices: 0.73 us -> 19.3 us
  other arithmetic: 15.9 us -> 30.7 us
    reduce_scatter x4 -> x1, waiting for transfers between devices: 204 us -> 0.01 us  [local(): lax.psum_scatter(down_cross, 'fsdp', scatter_dimension=0, tiled=True)]
    all_gather x6 -> x2, waiting for transfers between devices: 168 us -> 6.57 us  [the longest x1 6.56 us: local(): lax.all_gather(jnp.concatenate([up_weight, down_weight], axis=1), 'fsdp',...]
    ppermute x0 -> x17, waiting for transfers between devices: none -> 107 us  [swap(): return lax.ppermute(value, name, [(i, i ^ 1 << bit) for i in range(size)])]
    unnamed x14 -> x3, waiting for transfers between devices: 91.6 us -> 0.05 us
    psum x1 -> x0, blocking collectives: 40.6 us -> none  [local(): lax.psum((gain_terms, qkv_spread, up_spread), ('fsdp', 'tp'))]
    ppermute x0 -> x17, starting transfers between devices: none -> 19.2 us  [swap(): return lax.ppermute(value, name, [(i, i ^ 1 << bit) for i in range(size)])]
    convert_element_type x1 -> x9, other arithmetic: 1.78 us -> 13.9 us  [the longest x6 8.83 us: step(): self.value = value.astype(self.carry)]
    unnamed x56 -> x75, local copies, waits for them, and re-layouts: 20.7 us -> 10.3 us
  transfers between devices with their start and end apart: 12 -> 20, of which waited for: 11 -> 10; matrix products, arithmetic and copies ran while one was open for 16% -> 37% of each run, Pallas kernels for 5% -> 11%
where the time goes in v2:
time: 319 us; the launch traced here: 314 us
  waiting for transfers between devices  114 us (36%)
  matrix products  74.4 us (23%)
  Pallas kernels  36 us (11%)
  other arithmetic  30.7 us (10%)
  local copies, waits for them, and re-layouts  25 us (8%)
  starting transfers between devices  19.3 us (6%)
  between operations  14.8 us (5%)
    ppermute x17, waiting for transfers between devices, swap(): return lax.ppermute(value, name, [(i, i ^ 1 << bit) for i in range(size)])  107 us
    pallas_call x1, Pallas kernels, attention(): outs.append(run(j, j, j, bias, bias, bias, att_grad[at], *tables))  36 us
    ppermute x17, starting transfers between devices, swap(): return lax.ppermute(value, name, [(i, i ^ 1 << bit) for i in range(size)])  19.2 us
    dot_general x4, matrix products, cross(): lax.dot_general(left, right, FIRST, preferred_element_type=jnp.float32)  16.7 us
    dot_general x1, matrix products, local(): jnp.dot(after(grad_rows, down_cross), down_all, preferred_element_type=jn...  10.8 us
    dot_general x1, matrix products, local(): jnp.dot(second_norm, up_all, preferred_element_type=jnp.float32) + up_bias  10.4 us
    unnamed x75, local copies, waits for them, and re-layouts  10.3 us
    dot_general x1, matrix products, local(): lax.dot_general(after(pre_grad16, up.got), up_all, LAST, preferred_elemen...  9.52 us
  transfers between devices with their start and end apart: 20, of which 10 were waited for; matrix products, arithmetic and copies ran while one was open for 37% of the time, Pallas kernels for 11%

profile of v2, /device:TPU:0, one launch (start us, length us, event | category | flops | bytes accessed | tf_op | source)
XLA Modules:
  0.0 313.8 jit_solution(740709320316767798)
XLA Ops:
  7.2 0.9 copy.47
  8.2 1.6 pad_maximum_fusion.3
  9.8 1.9 pad_maximum_fusion.2
  11.7 3.0 collective-permute-start
  14.8 0.7 copy.50
  15.5 23.4 %collective-permute-done = bf16[512,1024]{1,0:T(8,128)(2,1)S(1)} collective-permute-done((bf16[512,1024]{1,0:T(8,128)(2,1)}, bf16[512,1024]{1,0:T(8,128)(2,1)S(1)}, u32[]{:S(2)}, u32[]{:S(2)}) %collective-permute-start) | collective-permute-done | bytes 1048608 | tf_op jit(solution)/shard_map/ppermute | solution.py:175
  38.9 21.6 %collective-permute-done.1 = bf16[512,1024]{1,0:T(8,128)(2,1)S(1)} collective-permute-done((bf16[512,1024]{1,0:T(8,128)(2,1)}, bf16[512,1024]{1,0:T(8,128)(2,1)S(1)}, u32[]{:S(2)}, u32[]{:S(2)}) %collective-permute-start.1) | collective-permute-done | bytes 1048608 | tf_op jit(solution)/shard_map/ppermute | solution.py:175
  60.6 1.9 select_bitcast_fusion.1
  62.8 0.7 multiply_reduce_fusion.2
  64.1 2.4 fusion.8
  66.5 2.6 convolution_convert_fusion.4.ag_ref
  69.1 1.1 copy-done.20
  70.3 3.4 %fusion.18.q_ref.k_ref.v_ref = f32[1024,1536]{1,0:T(8,128)S(1)} fusion(bf16[1024,2048]{1,0:T(8,128)(2,1)S(1)} %copy-done.20, f32[1024,1024]{1,0:T(8,128)S(1)} %copy-done.4, f32[1024]{0:T(1024)S(1)} %copy-done.25, f32[1024]{0:T(1024)S(1)} %copy-done.28), kind=kOutput, calls=%fused_computation.35 | convolution fusion | flops 3224371200 | bytes 13639680 | tf_op jit(solution)/shard_map/dot_general | solution.py:288
  73.7 36.0 %attention.1 = (bf16[1024,512]{1,0:T(8,128)(2,1)S(1)}, bf16[1024,1536]{1,0:T(8,128)(2,1)S(1)}, f32[3,1,512]{2,1,0:T(1,128)S(1)}) custom-call(f32[1024,1536]{1,0:T(8,128)S(1)} %fusion.18.q_ref.k_ref.v_ref, f32[1024,1536]{1,0:T(8,128)S(1)} %fusion.18.q_ref.k_ref.v_ref, f32[1024,1536]{1,0:T(8,128)S(1)} %fusion.18.q_ref.k_ref.v_ref, f32[1,1536]{1,0:T(1,128)S(1)} %bitcast.121, ...), custom_call_target="tpu_custom_call" | custom-call | flops 21474836480 | bytes 7340032 | tf_op jit(solution)/shard_map/attention/pallas_call | solution.py:159
  109.7 1.3 convolution_convert_fusion.3
  111.4 3.9 %convolution_convert_fusion = bf16[1024,1536]{1,0:T(8,128)(2,1)S(1)} fusion(bf16[1024,1536]{1,0:T(8,128)(2,1)S(1)} %get-tuple-element.33, f32[1024,1024]{1,0:T(8,128)S(1)} %copy-done.4, f32[1024]{0:T(1024)S(1)} %copy-done.25, f32[1024]{0:T(1024)S(1)} %copy-done.28), kind=kOutput, calls=%fused_computation.23 | convolution fusion | flops 3225944064 | bytes 10493952 | tf_op jit(solution)/shard_map/dot_general | solution.py:283
  115.9 1.6 constant_dynamic-slice_fusion.2
  117.5 1.6 copy.61
  119.4 8.4 %fusion.16 = f32[1024,1024]{1,0:T(8,128)} fusion(bf16[1024,1536]{1,0:T(8,128)(2,1)} %copy-done.3, bf16[1024,2048]{1,0:T(8,128)(2,1)} %all-gather.3.cloned.1.call-done), kind=kOutput, calls=%fused_computation.33 | convolution fusion | flops 3221225472 | bytes 10485760 | tf_op jit(solution)/shard_map/dot_general | solution.py:295
  127.8 2.5 fusion.7
  130.4 1.4 copy-done.12
  131.8 1.8 collective-permute-start.6
  133.6 6.6 %all-gather.5.cloned.1.call-done = bf16[1024,4096]{1,0:T(8,128)(2,1)} async-done(((bf16[64,4096]{1,0:T(8,128)(2,1)}), bf16[1024,4096]{1,0:T(8,128)(2,1)}) %all-gather.5.cloned.1.call-update) | async-done | bytes 8388624 | tf_op jit(solution)/shard_map/all_gather | solution.py:276
  140.2 10.4 %multiply_convert_fusion = (bf16[1024,2048]{1,0:T(8,128)(2,1)S(1)}, f32[1024,2048]{1,0:T(8,128)}) fusion(f32[2048]{0:T(1024)S(1)} %copy-done.24, bf16[1024,4096]{1,0:T(8,128)(2,1)} %all-gather.5.cloned.1.call-done, f32[1024,1024]{1,0:T(8,128)} %fusion.8, f32[1024]{0:T(1024)S(1)} %copy-done.26, f32[1024]{0:T(1024)S(1)} %copy-done.27), kind=kOutput, calls=%fused_computation.8 | convolution fusion | flops 4310695936 | bytes 20987904 | tf_op jit(solution)/shard_map/dot_general | solution.py:297
  150.6 2.1 copy-done.29
  152.6 6.3 %convolution_convert_fusion.2 = bf16[1024,2048]{1,0:T(8,128)(2,1)} fusion(bf16[1024,1024]{1,0:T(8,128)(2,1)S(1)} %bitcast.134, bf16[1024,2048]{1,0:T(8,128)(2,1)S(1)} %get-tuple-element.82), kind=kOutput, calls=%fused_computation.25 | convolution fusion | flops 4297064448 | bytes 10485760 | tf_op jit(solution)/shard_map/dot_general | solution.py:283
  158.9 10.8 %convert_reduce_fusion = (f32[2048]{0:T(1024)S(1)}, bf16[1024,2048]{1,0:T(8,128)(2,1)S(1)}) fusion(f32[1024,2048]{1,0:T(8,128)} %get-tuple-element.83, f32[2048]{0:T(1024)S(1)} %copy-done.24, bf16[1024,1024]{1,0:T(8,128)(2,1)} %bitcast.132, bf16[1024,4096]{1,0:T(8,128)(2,1)} %all-gather.5.cloned.1.call-done), kind=kOutput, calls=%fused_computation.7 | convolution fusion | flops 4322228224 | bytes 18890752 | tf_op jit(solution)/shard_map/dot_general | solution.py:306
  169.7 5.2 %convolution_convert_fusion.1 = bf16[1024,2048]{1,0:T(8,128)(2,1)S(1)} fusion(bf16[1024,2048]{1,0:T(8,128)(2,1)S(1)} %get-tuple-element.31, f32[1024,1024]{1,0:T(8,128)S(1)} %copy-done.5, f32[1024]{0:T(1024)S(1)} %copy-done.26, f32[1024]{0:T(1024)S(1)} %copy-done.27), kind=kOutput, calls=%fused_computation.24 | convolution fusion | flops 4300210176 | bytes 12591104 | tf_op jit(solution)/shard_map/dot_general | solution.py:283
  175.0 1.7 constant_dynamic-slice_fusion
  177.3 1.1 copy-done.13
  178.4 1.9 fusion.22
  180.4 1.1 collective-permute-start.7
  181.4 8.8 %fusion.9 = f32[1024,1024]{1,0:T(8,128)} fusion(bf16[1024,2048]{1,0:T(8,128)(2,1)S(1)} %copy-done.30, bf16[1024,4096]{1,0:T(8,128)(2,1)} %all-gather.5.cloned.1.call-done), kind=kOutput, calls=%fused_computation.26 | convolution fusion | flops 4294967296 | bytes 12582912 | tf_op jit(solution)/shard_map/dot_general | solution.py:321
  190.2 11.9 %collective-permute-done.7 = bf16[2,64,2048]{2,1,0:T(8,128)(2,1)S(1)} collective-permute-done((bf16[2,64,2048]{2,1,0:T(8,128)(2,1)S(1)}, bf16[2,64,2048]{2,1,0:T(8,128)(2,1)S(1)}, u32[]{:S(2)}, u32[]{:S(2)}) %collective-permute-start.7) | collective-permute-done | bytes 524320 | tf_op jit(solution)/shard_map/ppermute | solution.py:175
  202.3 0.8 copy-done.19
  203.1 1.2 collective-permute-start.8
  204.2 9.5 %fusion.38 = (f32[1024]{0:T(1024)S(1)}, f32[1024]{0:T(1024)S(1)}, f32[1024]{0:T(1024)S(1)}, f32[1024]{0:T(1024)S(1)}, f32[1024,1024]{1,0:T(8,128)}) fusion(f32[1024,1024]{1,0:T(8,128)S(1)} %copy-done.5, f32[1024,1024]{1,0:T(8,128)S(1)} %copy-done.31, f32[1024]{0:T(1024)S(1)} %copy-done.27, f32[1024]{0:T(1024)S(1)} %copy-done.28, ...), kind=kOutput, calls=%fused_computation.101 | convolution fusion | flops 4304400384 | bytes 20996096 | tf_op jit(solution)/shard_map/dot_general | solution.py:312
  213.9 3.8 %convolution_add_fusion = f32[1024,1024]{1,0:T(8,128)S(1)} fusion(f32[1024,1024]{1,0:T(8,128)} %fusion.9, bf16[1024,512]{1,0:T(8,128)(2,1)S(1)} %get-tuple-element.32, bf16[1024,2048]{1,0:T(8,128)(2,1)} %all-gather.3.cloned.1.call-done), kind=kOutput, calls=%fused_computation.39 | convolution fusion | flops 1074790400 | bytes 10485760 | tf_op jit(solution)/shard_map/dot_general | solution.py:318
  217.8 2.1 copy-done.7
  219.9 1.1 fusion.26
  221.1 2.7 fusion.27
  223.8 1.5 collective-permute-start.4
  225.8 0.8 collective-permute-start.10
  226.6 2.4 fusion.6
  229.0 1.4 collective-permute-done.10
  230.4 2.6 collective-permute-start.11
  233.1 1.1 dynamic-slice_bitcast_fusion
  234.2 0.8 collective-permute-start.14
  235.0 1.5 collective-permute-done.11
  236.9 4.9 %collective-permute-done.12 = f32[8704]{0:T(1024)S(1)} collective-permute-done((f32[8704]{0:T(1024)S(1)}, f32[8704]{0:T(1024)S(1)}, u32[]{:S(2)}, u32[]{:S(2)}) %collective-permute-start.12) | collective-permute-done | bytes 34848 | tf_op jit(solution)/shard_map/ppermute | solution.py:175
  241.8 1.1 collective-permute-start.13
  242.9 1.1 convert_add_fusion.8
  244.6 0.8 copy.63
  246.6 25.8 %collective-permute-done.13 = f32[5120]{0:T(1024)S(1)} collective-permute-done((f32[5120]{0:T(1024)S(1)}, f32[5120]{0:T(1024)S(1)}, u32[]{:S(2)}, u32[]{:S(2)}) %collective-permute-start.13) | collective-permute-done | bytes 20512 | tf_op jit(solution)/shard_map/ppermute | solution.py:175
  273.1 1.8 fusion.21
  274.9 2.5 collective-permute-start.15
  277.5 2.4 fusion.33
  279.9 3.0 fusion.20
  282.9 6.5 %collective-permute-done.15 = bf16[2,64,2048]{2,1,0:T(8,128)(2,1)S(1)} collective-permute-done((bf16[2,64,2048]{2,1,0:T(8,128)(2,1)S(1)}, bf16[2,64,2048]{2,1,0:T(8,128)(2,1)S(1)}, u32[]{:S(2)}, u32[]{:S(2)}) %collective-permute-start.15) | collective-permute-done | bytes 524320 | tf_op jit(solution)/shard_map/ppermute | solution.py:175
  289.5 1.4 collective-permute-start.16
  291.0 2.7 fusion.25
  293.7 9.9 %collective-permute-done.16 = bf16[64,2048]{1,0:T(8,128)(2,1)S(1)} collective-permute-done((bf16[64,2048]{1,0:T(8,128)(2,1)S(1)}, bf16[64,2048]{1,0:T(8,128)(2,1)S(1)}, u32[]{:S(2)}, u32[]{:S(2)}) %collective-permute-start.16) | collective-permute-done | bytes 262176 | tf_op jit(solution)/shard_map/ppermute | solution.py:175
  303.6 0.8 convert_add_fusion.7
  304.4 1.8 convert_element_type.216
  (127 shorter events, 7.7 us)
Async XLA Ops:
  7.2 59.3 %all-gather.3.cloned.1.call-start = ((), (), s32[]{:S(2)}) async-start(), calls=%async_computation.1 | async-start | bytes 4456448 | tf_op jit(solution)/shard_map/all_gather | solution.py:273
  9.8 130.4 %all-gather.5.cloned.1.call-start = ((), (), s32[]{:S(2)}) async-start(), calls=%async_computation.2 | async-start | bytes 8912896 | tf_op jit(solution)/shard_map/all_gather | solution.py:276
  11.7 292.8 %reduce-scatter.2.cloned.1.call-start = ((), (), s32[]{:S(2)}) async-start(), calls=%async_computation.3 | async-start | bytes 4456448 | tf_op jit(solution)/shard_map/reduce_scatter | solution.py:302
  11.7 27.2 %collective-permute-start = (bf16[512,1024]{1,0:T(8,128)(2,1)}, bf16[512,1024]{1,0:T(8,128)(2,1)S(1)}, u32[]{:S(2)}, u32[]{:S(2)}) collective-permute-start(bf16[512,1024]{1,0:T(8,128)(2,1)} %param.17), channel_id=1, source_target_pairs={{0,1},{1,0},{2,3},{3,2},{4,5},{5,4},{6,7},{7,6},{8,9},{9,8},{10,11... | collective-permute-start | bytes 3145736 | tf_op jit(solution)/shard_map/ppermute | solution.py:175
  14.7 45.8 %collective-permute-start.1 = (bf16[512,1024]{1,0:T(8,128)(2,1)}, bf16[512,1024]{1,0:T(8,128)(2,1)S(1)}, u32[]{:S(2)}, u32[]{:S(2)}) collective-permute-start(bf16[512,1024]{1,0:T(8,128)(2,1)} %param.18), channel_id=1, source_target_pairs={{0,1},{1,0},{2,3},{3,2},{4,5},{5,4},{6,7},{7,6},{8,9},{9,8},{10,11... | collective-permute-start | bytes 3145736 | tf_op jit(solution)/shard_map/ppermute | solution.py:175
  63.8 2.7 copy-start.16
  66.5 2.7 copy-start.4
  66.5 3.8 %copy-start.20 = (bf16[1024,2048]{1,0:T(8,128)(2,1)S(1)}, bf16[1024,2048]{1,0:T(8,128)(2,1)}, u32[]{:S(2)}) copy-start(bf16[1024,2048]{1,0:T(8,128)(2,1)} %all-gather.3.cloned.1.call-done) | copy-start | bytes 12582916
  66.5 3.8 %copy-start.25 = (f32[1024]{0:T(1024)S(1)}, f32[1024]{0:T(1024)}, u32[]{:S(2)}) copy-start(f32[1024]{0:T(1024)} %param.28) | copy-start | bytes 12292
  66.5 3.8 %copy-start.28 = (f32[1024]{0:T(1024)S(1)}, f32[1024]{0:T(1024)}, u32[]{:S(2)}) copy-start(f32[1024]{0:T(1024)} %param.27) | copy-start | bytes 12292
  70.3 3.4 %copy-start = (f32[1024,128]{1,0:T(8,128)S(1)}, f32[1024,128]{1,0:T(8,128)}, u32[]{:S(2)}) copy-start(f32[1024,128]{1,0:T(8,128)} %constant.102.clone.sb_ref) | copy-start | bytes 1572868
  70.3 3.5 %copy-start.1 = (f32[1024,128]{1,0:T(8,128)S(1)}, f32[1024,128]{1,0:T(8,128)}, u32[]{:S(2)}) copy-start(f32[1024,128]{1,0:T(8,128)} %constant.101.clone.sa_ref) | copy-start | bytes 1572868
  70.3 3.5 %copy-start.2 = (f32[1024,128]{1,0:T(8,128)S(1)}, f32[1024,128]{1,0:T(8,128)}, u32[]{:S(2)}) copy-start(f32[1024,128]{1,0:T(8,128)} %constant.100.clone.cos_ref) | copy-start | bytes 1572868
  73.7 36.0 %copy-start.17 = (bf16[2,512,1024]{2,1,0:T(8,128)(2,1)S(1)}, bf16[2,512,1024]{2,1,0:T(8,128)(2,1)}, u32[]{:S(2)}) copy-start(bf16[2,512,1024]{2,1,0:T(8,128)(2,1)} %copy-done.16) | copy-start | bytes 6291460
  109.7 1.6 copy-start.3
  117.5 1.6 copy-start.9
  119.2 8.6 %collective-permute-start.5 = (bf16[2,2,2,64,2048]{4,3,0,1,2:T(8,128)(2,1)}, bf16[2,2,2,64,2048]{4,3,0,1,2:T(8,128)(2,1)}, u32[]{:S(2)}, u32[]{:S(2)}) collective-permute-start(bf16[2,2,2,64,2048]{4,3,0,1,2:T(8,128)(2,1)} %bitcast.118), channel_id=1, source_target_pairs={{0,2},{2,0},{4,6},{6,4},{8,10},{10,8},{12,14},{14,12},{16,18},{18,... | collective-permute-start | bytes 6291464 | tf_op jit(solution)/shard_map/ppermute | solution.py:175
  119.4 8.4 %copy-start.11 = (bf16[2,2,2,1,64,2048]{5,4,3,2,1,0:T(8,128)(2,1)S(1)}, bf16[2,2,2,1,64,2048]{5,4,3,2,1,0:T(8,128)(2,1)}, u32[]{:S(2)}) copy-start(bf16[2,2,2,1,64,2048]{5,4,3,2,1,0:T(8,128)(2,1)} %get-tuple-element.67) | copy-start | bytes 6291460
  127.8 12.4 %copy-start.24 = (f32[2048]{0:T(1024)S(1)}, f32[2048]{0:T(1024)}, u32[]{:S(2)}) copy-start(f32[2048]{0:T(1024)} %param.24) | copy-start | bytes 24580
  127.8 12.4 %copy-start.26 = (f32[1024]{0:T(1024)S(1)}, f32[1024]{0:T(1024)}, u32[]{:S(2)}) copy-start(f32[1024]{0:T(1024)} %param.30) | copy-start | bytes 12292
  127.8 12.4 %copy-start.27 = (f32[1024]{0:T(1024)S(1)}, f32[1024]{0:T(1024)}, u32[]{:S(2)}) copy-start(f32[1024]{0:T(1024)} %param.29) | copy-start | bytes 12292
  130.3 1.4 copy-start.12
  131.8 27.1 %collective-permute-start.6 = (bf16[2,2,64,2048]{3,2,0,1:T(8,128)(2,1)S(1)}, bf16[2,2,64,2048]{3,2,0,1:T(8,128)(2,1)}, u32[]{:S(2)}, u32[]{:S(2)}) collective-permute-start(bf16[2,2,64,2048]{3,2,0,1:T(8,128)(2,1)S(1)} %dynamic-slice_bitcast_fusion.1), channel_id=1, source_target_pairs={{0,4},{2,6},{4,0},{6,2},{8,12},{10,14},{12,8},{14,10},{16,20},{18,... | collective-permute-start | bytes 3145736 | tf_op jit(solution)/shard_map/ppermute | solution.py:175
  140.2 12.4 %copy-start.18 = (bf16[2,512,1024]{2,1,0:T(8,128)(2,1)S(1)}, bf16[2,512,1024]{2,1,0:T(8,128)(2,1)}, u32[]{:S(2)}) copy-start(bf16[2,512,1024]{2,1,0:T(8,128)(2,1)} %copy-done.16) | copy-start | bytes 6291460
  150.6 2.1 copy-start.29
  158.9 10.8 %copy-start.5 = (f32[1024,1024]{1,0:T(8,128)S(1)}, f32[1024,1024]{1,0:T(8,128)}, u32[]{:S(2)}) copy-start(f32[1024,1024]{1,0:T(8,128)} %fusion.8) | copy-start | bytes 12582916
  169.7 5.3 %copy-start.32 = (bf16[1024,2048]{1,0:T(8,128)(2,1)}, bf16[1024,2048]{1,0:T(8,128)(2,1)S(1)}, u32[]{:S(2)}) copy-start(bf16[1024,2048]{1,0:T(8,128)(2,1)S(1)} %get-tuple-element.31) | copy-start | bytes 12582916
  176.7 1.6 copy-start.13
  176.7 4.7 %copy-start.30 = (bf16[1024,2048]{1,0:T(8,128)(2,1)S(1)}, bf16[1024,2048]{1,0:T(8,128)(2,1)}, u32[]{:S(2)}) copy-start(bf16[1024,2048]{1,0:T(8,128)(2,1)} %copy-done.29) | copy-start | bytes 12582916
  177.0 27.2 %collective-permute-start.2 = (bf16[2,2,2,64,2048]{4,3,0,1,2:T(8,128)(2,1)S(1)}, bf16[2,2,2,64,2048]{4,3,0,1,2:T(8,128)(2,1)}, u32[]{:S(2)}, u32[]{:S(2)}) collective-permute-start(bf16[2,2,2,64,2048]{4,3,0,1,2:T(8,128)(2,1)S(1)} %bitcast.135), channel_id=1, source_target_pairs={{0,2},{2,0},{4,6},{6,4},{8,10},{10,8},{12,14},{14,12},{16,18},{18,... | collective-permute-start | bytes 6291464 | tf_op jit(solution)/shard_map/ppermute | solution.py:175
  180.3 23.9 %slice-start = ((s8[8388608]{0:T(1024)(128)(4,1)}), s8[4194304]{0:T(1024)(128)(4,1)S(1)}, s32[]{:S(2)}) async-start(s8[8388608]{0:T(1024)(128)(4,1)} %bitcast.150), calls=%async_computation.4 | async-start | bytes 8388608
  180.3 23.9 %slice-start.1 = ((s8[8388608]{0:T(1024)(128)(4,1)}), s8[4194304]{0:T(1024)(128)(4,1)S(1)}, s32[]{:S(2)}) async-start(s8[8388608]{0:T(1024)(128)(4,1)} %bitcast.150), calls=%async_computation.5 | async-start | bytes 8388608
  180.4 23.9 %copy-start.31 = (f32[1024,1024]{1,0:T(8,128)S(1)}, f32[1024,1024]{1,0:T(8,128)}, u32[]{:S(2)}) copy-start(f32[1024,1024]{1,0:T(8,128)} %fusion.16) | copy-start | bytes 12582916
  180.4 21.7 %collective-permute-start.7 = (bf16[2,64,2048]{2,1,0:T(8,128)(2,1)S(1)}, bf16[2,64,2048]{2,1,0:T(8,128)(2,1)S(1)}, u32[]{:S(2)}, u32[]{:S(2)}) collective-permute-start(bf16[2,64,2048]{2,1,0:T(8,128)(2,1)S(1)} %dynamic-slice_bitcast_fusion.3), channel_id=1, source_target_pairs={{0,8},{2,10},{4,12},{6,14},{8,0},{10,2},{12,4},{14,6},{16,24},{18,... | collective-permute-start | bytes 1572872 | tf_op jit(solution)/shard_map/ppermute | solution.py:175
  202.2 0.8 copy-start.19
  203.1 33.8 %collective-permute-start.8 = (bf16[64,2048]{1,0:T(8,128)(2,1)S(1)}, bf16[64,2048]{1,0:T(8,128)(2,1)}, u32[]{:S(2)}, u32[]{:S(2)}) collective-permute-start(bf16[64,2048]{1,0:T(8,128)(2,1)S(1)} %dynamic-slice_bitcast_fusion.5), channel_id=1, source_target_pairs={{0,16},{2,18},{4,20},{6,22},{8,24},{10,26},{12,28},{14,30},{16,0},... | collective-permute-start | bytes 786440 | tf_op jit(solution)/shard_map/ppermute | solution.py:175
  213.8 12.0 %collective-permute-start.9 = (f32[8704]{0:T(1024)S(1)}, f32[8704]{0:T(1024)S(1)}, u32[]{:S(2)}, u32[]{:S(2)}) collective-permute-start(f32[8704]{0:T(1024)S(1)} %pad_maximum_fusion.4), channel_id=1, source_target_pairs={{0,2},{2,0},{4,6},{6,4},{8,10},{10,8},{12,14},{14,12},{16,18},{18,... | collective-permute-start | bytes 104456 | tf_op jit(solution)/shard_map/ppermute | solution.py:175
  217.8 2.1 copy-start.7
  217.8 8.8 %copy-start.10 = (bf16[2,2,2,1,64,2048]{5,4,3,2,1,0:T(8,128)(2,1)S(1)}, bf16[2,2,2,1,64,2048]{5,4,3,2,1,0:T(8,128)(2,1)}, u32[]{:S(2)}) copy-start(bf16[2,2,2,1,64,2048]{5,4,3,2,1,0:T(8,128)(2,1)} %get-tuple-element.65) | copy-start | bytes 6291460
  223.8 49.3 %collective-permute-start.4 = (bf16[512,1024]{1,0:T(8,128)(2,1)}, bf16[512,1024]{1,0:T(8,128)(2,1)}, u32[]{:S(2)}, u32[]{:S(2)}) collective-permute-start(bf16[512,1024]{1,0:T(8,128)(2,1)} %fusion.27), channel_id=1, source_target_pairs={{0,1},{1,0},{2,3},{3,2},{4,5},{5,4},{6,7},{7,6},{8,9},{9,8},{10,11... | collective-permute-start | bytes 3145736 | tf_op jit(solution)/shard_map/ppermute | solution.py:175
  225.3 47.8 %collective-permute-start.3 = (bf16[512,1024]{1,0:T(8,128)(2,1)}, bf16[512,1024]{1,0:T(8,128)(2,1)}, u32[]{:S(2)}, u32[]{:S(2)}) collective-permute-start(bf16[512,1024]{1,0:T(8,128)(2,1)} %fusion.26), channel_id=1, source_target_pairs={{0,1},{1,0},{2,3},{3,2},{4,5},{5,4},{6,7},{7,6},{8,9},{9,8},{10,11... | collective-permute-start | bytes 3145736 | tf_op jit(solution)/shard_map/ppermute | solution.py:175
  225.8 4.6 %collective-permute-start.10 = (f32[8704]{0:T(1024)S(1)}, f32[8704]{0:T(1024)S(1)}, u32[]{:S(2)}, u32[]{:S(2)}) collective-permute-start(f32[8704]{0:T(1024)S(1)} %fusion.37), channel_id=1, source_target_pairs={{0,4},{2,6},{4,0},{6,2},{8,12},{10,14},{12,8},{14,10},{16,20},{18,... | collective-permute-start | bytes 104456 | tf_op jit(solution)/shard_map/ppermute | solution.py:175
  226.6 8.3 %copy-start.22 = (f32[1024]{0:T(1024)S(1)}, f32[1024]{0:T(1024)}, u32[]{:S(2)}) copy-start(f32[1024]{0:T(1024)} %param.22) | copy-start | bytes 12292
  226.6 8.3 %copy-start.23 = (f32[1024]{0:T(1024)S(1)}, f32[1024]{0:T(1024)}, u32[]{:S(2)}) copy-start(f32[1024]{0:T(1024)} %param.26) | copy-start | bytes 12292
  230.4 6.1 %collective-permute-start.11 = (f32[8704]{0:T(1024)S(1)}, f32[8704]{0:T(1024)S(1)}, u32[]{:S(2)}, u32[]{:S(2)}) collective-permute-start(f32[8704]{0:T(1024)S(1)} %add.206), channel_id=1, source_target_pairs={{0,8},{2,10},{4,12},{6,14},{8,0},{10,2},{12,4},{14,6},{16,24},{18,... | collective-permute-start | bytes 104456 | tf_op jit(solution)/shard_map/ppermute | solution.py:175
  234.2 38.9 %collective-permute-start.14 = (bf16[2,2,64,2048]{3,2,0,1:T(8,128)(2,1)}, bf16[2,2,64,2048]{3,2,0,1:T(8,128)(2,1)}, u32[]{:S(2)}, u32[]{:S(2)}) collective-permute-start(bf16[2,2,64,2048]{3,2,0,1:T(8,128)(2,1)} %dynamic-slice_bitcast_fusion), channel_id=1, source_target_pairs={{0,4},{2,6},{4,0},{6,2},{8,12},{10,14},{12,8},{14,10},{16,20},{18,... | collective-permute-start | bytes 3145736 | tf_op jit(solution)/shard_map/ppermute | solution.py:175
  236.5 5.3 %collective-permute-start.12 = (f32[8704]{0:T(1024)S(1)}, f32[8704]{0:T(1024)S(1)}, u32[]{:S(2)}, u32[]{:S(2)}) collective-permute-start(f32[8704]{0:T(1024)S(1)} %add.207), channel_id=1, source_target_pairs={{0,16},{2,18},{4,20},{6,22},{8,24},{10,26},{12,28},{14,30},{16,0},... | collective-permute-start | bytes 104456 | tf_op jit(solution)/shard_map/ppermute | solution.py:175
  241.8 30.7 %collective-permute-start.13 = (f32[5120]{0:T(1024)S(1)}, f32[5120]{0:T(1024)S(1)}, u32[]{:S(2)}, u32[]{:S(2)}) collective-permute-start(f32[5120]{0:T(1024)S(1)} %slice.80), channel_id=1, source_target_pairs={{0,1},{1,0},{2,3},{3,2},{4,5},{5,4},{6,7},{7,6},{8,9},{9,8},{10,11... | collective-permute-start | bytes 61448 | tf_op jit(solution)/shard_map/ppermute | solution.py:175
  246.6 30.8 %copy-start.6 = (f32[1024,1024]{1,0:T(8,128)S(1)}, f32[1024,1024]{1,0:T(8,128)}, u32[]{:S(2)}) copy-start(f32[1024,1024]{1,0:T(8,128)} %fusion.8) | copy-start | bytes 12582916
  273.1 33.2 %copy-start.21 = (f32[1024]{0:T(1024)}, f32[1024]{0:T(1024)S(1)}, u32[]{:S(2)}) copy-start(f32[1024]{0:T(1024)S(1)} %get-tuple-element.118) | copy-start | bytes 12292
  273.1 6.8 %copy-start.14 = (f32[1024,1024]{1,0:T(8,128)S(1)}, f32[1024,1024]{1,0:T(8,128)}, u32[]{:S(2)}) copy-start(f32[1024,1024]{1,0:T(8,128)} %get-tuple-element.64) | copy-start | bytes 12582916
  274.9 14.5 %collective-permute-start.15 = (bf16[2,64,2048]{2,1,0:T(8,128)(2,1)S(1)}, bf16[2,64,2048]{2,1,0:T(8,128)(2,1)S(1)}, u32[]{:S(2)}, u32[]{:S(2)}) collective-permute-start(bf16[2,64,2048]{2,1,0:T(8,128)(2,1)S(1)} %dynamic-slice_bitcast_fusion.2), channel_id=1, source_target_pairs={{0,8},{2,10},{4,12},{6,14},{8,0},{10,2},{12,4},{14,6},{16,24},{18,... | collective-permute-start | bytes 1572872 | tf_op jit(solution)/shard_map/ppermute | solution.py:175
  279.9 11.1 %copy-start.8 = (f32[1024,1024]{1,0:T(8,128)S(1)}, f32[1024,1024]{1,0:T(8,128)}, u32[]{:S(2)}) copy-start(f32[1024,1024]{1,0:T(8,128)} %copy-done.7) | copy-start | bytes 12582916
  279.9 11.1 %copy-start.15 = (bf16[512,1024]{1,0:T(8,128)(2,1)S(1)}, bf16[512,1024]{1,0:T(8,128)(2,1)}, u32[]{:S(2)}) copy-start(bf16[512,1024]{1,0:T(8,128)(2,1)} %param.17) | copy-start | bytes 3145732
  289.5 14.1 %collective-permute-start.16 = (bf16[64,2048]{1,0:T(8,128)(2,1)S(1)}, bf16[64,2048]{1,0:T(8,128)(2,1)S(1)}, u32[]{:S(2)}, u32[]{:S(2)}) collective-permute-start(bf16[64,2048]{1,0:T(8,128)(2,1)S(1)} %dynamic-slice_bitcast_fusion.4), channel_id=1, source_target_pairs={{0,16},{2,18},{4,20},{6,22},{8,24},{10,26},{12,28},{14,30},{16,0},... | collective-permute-start | bytes 786440 | tf_op jit(solution)/shard_map/ppermute | solution.py:175
Sparse Core Ops, SparseCore 0:
  10.7 53.2 all-gather.2
  66.8 73.3 all-gather.4
  159.0 82.7 reduce-scatter.1
